TPU v7x, 512 devices: a whole 4x8x8 slice. The times are simulated.
512 devices in a mesh: seq: 32 (over x, y), dp: 16 (over z, core).
Axes of the slice: x: 4, y: 8, z: 8, core: 2. Of those that a mesh axis runs over, the one named last changes fastest.
Arguments:
- input_rows: bfloat16 [16, 8192, 768], P('dp', 'seq'), may hold values from -6 to 6
- features: bfloat16 [16, 4096, 768], P('dp', 'seq'), may hold values from -36 to 36
- norm_gain: float32 [768], replicated, may hold values from 0.1 to 1.9
- w_query: bfloat16 [768, 512], replicated, may hold values from -3 to 3
- w_key: bfloat16 [768, 512], replicated, may hold values from -3 to 3
- w_value: bfloat16 [768, 512], replicated, may hold values from -0.21875 to 0.21875
- temper: float32 [4], replicated, may hold values from 1 to 4
- head_grads: bfloat16 [16, 4096, 512], P('dp', 'seq'), may hold values from -6 to 6
Outputs:
- feature_grad: bfloat16 [16, 4096, 768], P('dp', 'seq')
- conv_grad: float32 [3, 768, 768], P(None, 'seq')
All inputs are finite; a program needn't handle non-finite values.
Results may differ from a plain program's by a relative error of at most 0.033.
Values may be sent and summed in bfloat16 or wider, within the bound.
A program may use at most 64 MiB of HBM per device.

v0:
```python
import math

import jax
import jax.numpy as jnp
from jax import lax
from jax.sharding import PartitionSpec as P

EPSILON = 1e-06
LAST_BOTH = (((1,), (1,)), ((), ()))
FIRST_BOTH = (((0,), (0,)), ((), ()))


def passed_along(value, axis, by):
    length = lax.axis_size(axis)
    pairs = [(i, i + by) for i in range(length) if 0 <= i + by < length]
    return lax.ppermute(value, axis, pairs)


def unit_rows(raw_vals):
    inv_scale = lax.rsqrt(jnp.mean(raw_vals * raw_vals, axis=-1, keepdims=True) + EPSILON)
    return (raw_vals * inv_scale, inv_scale)


def unit_back(upstream, unit_vals, inv_scale):
    return inv_scale * (
        upstream - unit_vals * jnp.mean(unit_vals * upstream, axis=-1, keepdims=True)
    )


def to_slots(stacked):
    return stacked.reshape((stacked.shape[0] * stacked.shape[1],) + stacked.shape[2:])


def from_slots(received, head_count, block_count):
    return received.reshape((head_count, block_count) + received.shape[1:])


def attend(queries, keys_all, values, upstream, factor):
    row_count = queries.shape[0]
    step_rows = min(512, row_count)
    step_count = row_count // step_rows

    def one_block(running, pieces):
        query_rows, upstream_rows = pieces
        scores = (
            lax.dot_general(query_rows, keys_all, LAST_BOTH, preferred_element_type=jnp.float32)
            * factor
        )
        expo_vals = jnp.exp(scores)
        attn_prob = expo_vals / jnp.sum(expo_vals, axis=1, keepdims=True)
        prob_low = attn_prob.astype(jnp.bfloat16)
        grad_prob = lax.dot_general(
            upstream_rows, values, LAST_BOTH, preferred_element_type=jnp.float32
        )
        grad_dot = jnp.sum(attn_prob * grad_prob, axis=1, keepdims=True)
        grad_score = (attn_prob * (grad_prob - grad_dot) * factor).astype(jnp.bfloat16)
        grad_query = jnp.dot(grad_score, keys_all, preferred_element_type=jnp.float32)
        grad_key = running[0] + lax.dot_general(
            grad_score, query_rows, FIRST_BOTH, preferred_element_type=jnp.float32
        )
        grad_value = running[1] + lax.dot_general(
            prob_low, upstream_rows, FIRST_BOTH, preferred_element_type=jnp.float32
        )
        return ((grad_key, grad_value), grad_query)

    zero_keys = jnp.zeros(keys_all.shape, jnp.float32)
    blocked = (
        queries.reshape(step_count, step_rows, -1),
        upstream.reshape(step_count, step_rows, -1),
    )
    (grad_key, grad_value), grad_query = lax.scan(one_block, (zero_keys, zero_keys), blocked)
    return (grad_query.reshape(row_count, -1), grad_key, grad_value)


def on_device(input_rows, features, norm_gain, w_query, w_key, w_value, temper, head_grads):
    head_count = temper.shape[0]
    head_size = w_query.shape[1] // head_count
    slot_count = lax.axis_size("seq")
    block_count = slot_count // head_count
    tokens = features.shape[1]
    span_rows = tokens // block_count
    channels = features.shape[2]
    batch_count = lax.axis_size("dp")
    feat_vals = features[0].astype(jnp.float32)
    inv_rms = lax.rsqrt(jnp.mean(feat_vals * feat_vals, axis=1, keepdims=True) + EPSILON)
    normed = (feat_vals * inv_rms * norm_gain).astype(jnp.bfloat16)
    q_raw = jnp.dot(normed, w_query, preferred_element_type=jnp.float32).reshape(
        tokens, head_count, head_size
    )
    k_raw = jnp.dot(normed, w_key, preferred_element_type=jnp.float32).reshape(
        tokens, head_count, head_size
    )
    q_unit, q_scale = unit_rows(q_raw)
    k_unit, k_scale = unit_rows(k_raw)
    queries = q_unit.astype(jnp.bfloat16)
    keys_own = k_unit.astype(jnp.bfloat16)
    values = jnp.dot(normed, w_value, preferred_element_type=jnp.float32).astype(jnp.bfloat16)
    values = values.reshape(tokens, head_count, head_size)
    upstream = head_grads[0].reshape(tokens, head_count, head_size)

    def split_rows(tensor):
        grouped = tensor.reshape(block_count, span_rows, head_count, head_size)
        return to_slots(jnp.transpose(grouped, (2, 0, 1, 3)))

    def copy_rows(tensor):
        heads_first = jnp.transpose(tensor, (1, 0, 2))
        spread = jnp.broadcast_to(
            heads_first[:, None], (head_count, block_count, tokens, head_size)
        )
        return to_slots(spread)

    q_in, up_in, k_in, v_in = (
        lax.all_to_all(split_rows(queries), "seq", split_axis=0, concat_axis=0, tiled=True),
        lax.all_to_all(split_rows(upstream), "seq", split_axis=0, concat_axis=0, tiled=True),
        lax.all_to_all(copy_rows(keys_own), "seq", split_axis=0, concat_axis=0, tiled=True),
        lax.all_to_all(copy_rows(values), "seq", split_axis=0, concat_axis=0, tiled=True),
    )
    own_slot = lax.axis_index("seq")
    own_head = own_slot // block_count
    factor = jnp.sum(jnp.where(jnp.arange(head_count) == own_head, temper, 0.0)) * (
        1.0 / math.sqrt(head_size)
    )
    grad_query, grad_key, grad_value = attend(
        q_in.reshape(-1, head_size),
        k_in.reshape(-1, head_size),
        v_in.reshape(-1, head_size),
        up_in.reshape(-1, head_size),
        factor,
    )
    dq_back, dk_back, dv_back = (
        lax.all_to_all(
            grad_query.astype(jnp.bfloat16).reshape(slot_count, span_rows, head_size),
            "seq",
            split_axis=0,
            concat_axis=0,
            tiled=True,
        ),
        lax.all_to_all(
            grad_key.astype(jnp.bfloat16).reshape(slot_count, tokens, head_size),
            "seq",
            split_axis=0,
            concat_axis=0,
            tiled=True,
        ),
        lax.all_to_all(
            grad_value.astype(jnp.bfloat16).reshape(slot_count, tokens, head_size),
            "seq",
            split_axis=0,
            concat_axis=0,
            tiled=True,
        ),
    )
    grad_q = jnp.transpose(from_slots(dq_back, head_count, block_count), (1, 2, 0, 3))
    grad_q = grad_q.reshape(tokens, head_count, head_size).astype(jnp.float32)
    key_sums = jnp.sum(from_slots(dk_back, head_count, block_count).astype(jnp.float32), axis=1)
    value_sums = jnp.sum(from_slots(dv_back, head_count, block_count).astype(jnp.float32), axis=1)
    grad_k = jnp.transpose(key_sums, (1, 0, 2))
    grad_v = jnp.transpose(value_sums, (1, 0, 2))
    dq_raw = (
        unit_back(grad_q, q_unit, q_scale)
        .astype(jnp.bfloat16)
        .reshape(tokens, head_count * head_size)
    )
    dk_raw = (
        unit_back(grad_k, k_unit, k_scale)
        .astype(jnp.bfloat16)
        .reshape(tokens, head_count * head_size)
    )
    dv_low = grad_v.astype(jnp.bfloat16).reshape(tokens, head_count * head_size)
    grad_normed = lax.dot_general(dq_raw, w_query, LAST_BOTH, preferred_element_type=jnp.float32)
    grad_normed = grad_normed + lax.dot_general(
        dk_raw, w_key, LAST_BOTH, preferred_element_type=jnp.float32
    )
    grad_normed = grad_normed + lax.dot_general(
        dv_low, w_value, LAST_BOTH, preferred_element_type=jnp.float32
    )
    gained = grad_normed * norm_gain
    unit_feats = feat_vals * inv_rms
    feature_grad = inv_rms * (
        gained - unit_feats * jnp.mean(unit_feats * gained, axis=1, keepdims=True)
    )
    feature_grad = feature_grad.astype(jnp.bfloat16)
    own_rows = input_rows[0]
    previous_row = passed_along(own_rows[-1:], "seq", 1)
    padded = jnp.concatenate(
        [previous_row, own_rows, jnp.zeros((1, channels), own_rows.dtype)], axis=0
    )
    row_pairs = padded.reshape(tokens + 1, 2, channels)
    windows = jnp.concatenate([row_pairs[:-1, 0], row_pairs[:-1, 1], row_pairs[1:, 0]], axis=1)
    weight_term = lax.dot_general(
        windows, feature_grad, FIRST_BOTH, preferred_element_type=jnp.float32
    )
    weight_term = (weight_term * (1.0 / batch_count)).reshape(3, channels, channels)
    partial_value = lax.psum_scatter(
        weight_term.astype(jnp.bfloat16), "seq", scatter_dimension=1, tiled=True
    )
    conv_grad = lax.psum(partial_value, "dp").astype(jnp.float32)
    return (feature_grad[None], conv_grad)


def solution(mesh):
    return jax.shard_map(
        on_device,
        mesh=mesh,
        in_specs=(
            P("dp", "seq", None),
            P("dp", "seq", None),
            P(),
            P(),
            P(),
            P(),
            P(),
            P("dp", "seq", None),
        ),
        out_specs=(P("dp", "seq", None), P(None, "seq", None)),
        check_vma=False,
    )
```

profile of v0, /device:TPU:1, one launch (start us, length us, event | category | flops | bytes accessed | tf_op | source)
XLA Modules:
  0.0 551.5 jit_solution(663431619319408128)
XLA Ops:
  7.2 1.1 fusion.23
  8.3 1.4 copy.59
  9.8 1.4 multiply_reduce_fusion.2
  11.2 0.7 copy-done.4
  11.9 0.8 copy.50
  12.6 10.5 %all-to-all-start = ((bf16[32,16,128]{2,1,0:T(8,128)(2,1)}), bf16[32,16,128]{2,1,0:T(8,128)(2,1)S(1)}, u32[]{:S(2)}, u32[]{:S(2)}) async-start(bf16[32,16,128]{2,1,0:T(8,128)(2,1)} %bitcast.7), calls=%async_computation | async-start | bytes 262144 | tf_op jit(solution)/shard_map/all_to_all | solution.py:113
  23.2 1.4 copy.60
  24.6 0.9 reshape_reshape_squeeze.3
  25.5 0.7 copy.54
  26.2 1.4 multiply_reduce_fusion.1
  27.6 4.7 all-to-all-done
  32.3 4.5 all-to-all-start.3
  37.0 9.0 %all-to-all-done.3 = bf16[32,16,128]{2,1,0:T(8,128)(2,1)S(1)} async-done(((bf16[32,16,128]{2,1,0:T(8,128)(2,1)}), bf16[32,16,128]{2,1,0:T(8,128)(2,1)S(1)}, u32[]{:S(2)}, u32[]{:S(2)}) %all-to-all-start.3) | async-done | bytes 131104 | tf_op jit(solution)/shard_map/all_to_all | solution.py:114
  46.0 1.2 broadcast_in_dim.15
  47.2 3.9 all-to-all-start.1
  51.2 0.3 convolution_convert_fusion.3
  51.6 23.2 %all-to-all-done.1 = bf16[32,128,128]{2,1,0:T(8,128)(2,1)S(1)} async-done(((bf16[32,128,128]{2,1,0:T(8,128)(2,1)}), bf16[32,128,128]{2,1,0:T(8,128)(2,1)S(1)}, u32[]{:S(2)}, u32[]{:S(2)}) %all-to-all-start.1) | async-done | bytes 1048608 | tf_op jit(solution)/shard_map/all_to_all | solution.py:115
  74.8 1.3 broadcast_in_dim.18
  76.1 7.5 %all-to-all-start.2 = ((bf16[32,128,128]{2,1,0:T(8,128)(2,1)}), bf16[32,128,128]{2,1,0:T(8,128)(2,1)S(1)}, u32[]{:S(2)}, u32[]{:S(2)}) async-start(bf16[32,128,128]{2,1,0:T(8,128)(2,1)} %bitcast.16), calls=%async_computation.2 | async-start | bytes 2097152 | tf_op jit(solution)/shard_map/all_to_all | solution.py:116
  83.6 0.6 fusion.38
  84.9 4.5 fusion.5
  89.4 15.8 %all-to-all-done.2 = bf16[32,128,128]{2,1,0:T(8,128)(2,1)S(1)} async-done(((bf16[32,128,128]{2,1,0:T(8,128)(2,1)}), bf16[32,128,128]{2,1,0:T(8,128)(2,1)S(1)}, u32[]{:S(2)}, u32[]{:S(2)}) %all-to-all-start.2) | async-done | bytes 1048608 | tf_op jit(solution)/shard_map/all_to_all | solution.py:116
  105.2 5.3 fusion
  110.5 0.5 copy-done.1
  111.0 3.0 fusion.3
  114.0 1.9 copy-done.2
  116.0 1.9 convolution_convert_fusion.2
  117.9 8.7 %all-to-all-start.4 = ((bf16[32,16,128]{2,1,0:T(8,128)(2,1)}), bf16[32,16,128]{2,1,0:T(8,128)(2,1)S(1)}, u32[]{:S(2)}, u32[]{:S(2)}) async-start(bf16[32,16,128]{2,1,0:T(8,128)(2,1)} %convolution_convert_fusion.2), calls=%async_computation.4 | async-start | bytes 262144 | tf_op jit(solution)/shard_map/all_to_all | solution.py:131
  126.6 4.5 convolution_convert_fusion.1
  131.1 4.6 all-to-all-done.4
  135.7 0.7 copy-done.6
  136.4 4.6 all-to-all-start.5
  141.0 3.3 collective-permute-start
  144.4 11.8 %collective-permute-done = bf16[1,768]{1,0:T(2,128)(2,1)S(1)} collective-permute-done((bf16[1,768]{1,0:T(2,128)(2,1)S(1)}, bf16[1,768]{1,0:T(2,128)(2,1)S(1)}, u32[]{:S(2)}, u32[]{:S(2)}) %collective-permute-start) | collective-permute-done | bytes 1568 | tf_op jit(solution)/shard_map/ppermute | solution.py:16
  156.2 0.1 maximum_maximum_fusion
  156.3 0.5 reshape.155
  156.8 6.3 %convolution_convert_fusion = bf16[4096,128]{1,0:T(8,128)(2,1)} fusion(bf16[512,128]{1,0:T(8,128)(2,1)S(1)} %bitcast.160, f32[512,4096]{1,0:T(8,128)} %get-tuple-element.39, f32[512]{0:T(512)S(1)} %get-tuple-element.38, f32[]{:T(128)S(6)} %mul.161), kind=kOutput, calls=%fused_computation.10 | convolution fusion | flops 543686656 | bytes 9570308 | tf_op jit(solution)/shard_map/while/body/eval_jaxpr/dot_general | solution.py:61
  163.2 12.7 %all-to-all-start.6 = ((bf16[32,128,128]{2,1,0:T(8,128)(2,1)}), bf16[32,128,128]{2,1,0:T(8,128)(2,1)S(1)}, u32[]{:S(2)}, u32[]{:S(2)}) async-start(bf16[32,128,128]{2,1,0:T(8,128)(2,1)} %bitcast.146), calls=%async_computation.6 | async-start | bytes 2097152 | tf_op jit(solution)/shard_map/all_to_all | solution.py:145
  176.0 0.7 fusion.42
  176.7 0.7 copy.70
  177.4 0.8 copy_bitcast_fusion
  178.2 1.6 convert.7
  179.8 1.1 copy.56
  180.9 1.0 multiply_reduce_fusion
  181.9 1.0 multiply_convert_fusion.1
  182.9 1.5 fusion.43
  184.4 0.8 convert_reduce_fusion
  185.2 1.1 copy.57
  186.3 1.0 fusion.26
  187.3 1.0 fusion.28
  188.3 7.2 %all-to-all-done.6 = bf16[32,128,128]{2,1,0:T(8,128)(2,1)S(1)} async-done(((bf16[32,128,128]{2,1,0:T(8,128)(2,1)}), bf16[32,128,128]{2,1,0:T(8,128)(2,1)S(1)}, u32[]{:S(2)}, u32[]{:S(2)}) %all-to-all-start.6) | async-done | bytes 1048608 | tf_op jit(solution)/shard_map/all_to_all | solution.py:145
  195.5 0.1 bitcast_reduce_fusion
  195.7 0.1 copy.58
  195.8 1.5 convolution_add_fusion.1
  197.4 0.5 fusion.19
  197.8 0.2 fusion.22
  198.0 2.3 multiply_convert_fusion
  200.3 3.0 copy.61
  203.4 2.5 copy.66
  206.0 218.8 %reduce-scatter.4.cloned.1.call-done = bf16[24,2304]{1,0:T(8,128)(2,1)} async-done(((bf16[768,2304]{1,0:T(8,128)(2,1)}), bf16[24,2304]{1,0:T(8,128)(2,1)}) %reduce-scatter.4.cloned.1.call-update) | async-done | bytes 110608
  424.8 0.9 reshape.163
  425.7 0.7 copy.62
  426.4 116.7 %all-reduce.2.cloned.1.call-done = bf16[3,24,768]{2,1,0:T(8,128)(2,1)} async-done(((bf16[3,24,768]{2,1,0:T(8,128)(2,1)}), bf16[3,24,768]{2,1,0:T(8,128)(2,1)}) %all-reduce.2.cloned.1.call-update) | async-done | bytes 110608 | tf_op jit(solution)/shard_map/psum | solution.py:197
  543.1 1.6 convert_element_type.124
  (40 shorter events, 0.5 us)
Async XLA Ops:
  7.2 44.0 %copy-start = (bf16[768,512]{1,0:T(8,128)(2,1)S(1)}, bf16[768,512]{1,0:T(8,128)(2,1)}, u32[]{:S(2)}) copy-start(bf16[768,512]{1,0:T(8,128)(2,1)} %param.13) | copy-start | bytes 2359300
  7.2 44.0 %copy-start.3 = (bf16[1,128,768]{2,1,0:T(8,128)(2,1)S(1)}, bf16[1,128,768]{2,1,0:T(8,128)(2,1)}, u32[]{:S(2)}) copy-start(bf16[1,128,768]{2,1,0:T(8,128)(2,1)} %param.9) | copy-start | bytes 589828
  7.2 44.0 %copy-start.11 = (f32[768]{0:T(1024)S(1)}, f32[768]{0:T(1024)}, u32[]{:S(2)}) copy-start(f32[768]{0:T(1024)} %param.10) | copy-start | bytes 9220
  7.2 76.4 %copy-start.12 = (f32[4]{0:T(128)S(1)}, f32[4]{0:T(128)}, u32[]{:S(2)}) copy-start(f32[4]{0:T(128)} %param.14) | copy-start | bytes 52
  11.2 0.7 copy-start.4
  12.6 19.7 %all-to-all-start = ((bf16[32,16,128]{2,1,0:T(8,128)(2,1)}), bf16[32,16,128]{2,1,0:T(8,128)(2,1)S(1)}, u32[]{:S(2)}, u32[]{:S(2)}) async-start(bf16[32,16,128]{2,1,0:T(8,128)(2,1)} %bitcast.7), calls=%async_computation | async-start | bytes 262144 | tf_op jit(solution)/shard_map/all_to_all | solution.py:113
  27.6 19.6 %copy-start.5 = (f32[128,4,128]{0,2,1:T(8,128)}, f32[128,4,128]{0,2,1:T(8,128)S(1)}, u32[]{:S(2)}) copy-start(f32[128,4,128]{0,2,1:T(8,128)S(1)} %get-tuple-element.37) | copy-start | bytes 786436
  32.3 13.7 %all-to-all-start.3 = ((bf16[32,16,128]{2,1,0:T(8,128)(2,1)}), bf16[32,16,128]{2,1,0:T(8,128)(2,1)S(1)}, u32[]{:S(2)}, u32[]{:S(2)}) async-start(bf16[32,16,128]{2,1,0:T(8,128)(2,1)} %bitcast.19), calls=%async_computation.3 | async-start | bytes 262144 | tf_op jit(solution)/shard_map/all_to_all | solution.py:114
  46.0 59.1 %copy-start.9 = (bf16[32,16,128]{2,1,0:T(8,128)(2,1)}, bf16[32,16,128]{2,1,0:T(8,128)(2,1)S(1)}, u32[]{:S(2)}) copy-start(bf16[32,16,128]{2,1,0:T(8,128)(2,1)S(1)} %all-to-all-done.3) | copy-start | bytes 393220
  47.2 27.5 %all-to-all-start.1 = ((bf16[32,128,128]{2,1,0:T(8,128)(2,1)}), bf16[32,128,128]{2,1,0:T(8,128)(2,1)S(1)}, u32[]{:S(2)}, u32[]{:S(2)}) async-start(bf16[32,128,128]{2,1,0:T(8,128)(2,1)} %bitcast.13), calls=%async_computation.1 | async-start | bytes 2097152 | tf_op jit(solution)/shard_map/all_to_all | solution.py:115
  76.1 29.1 %all-to-all-start.2 = ((bf16[32,128,128]{2,1,0:T(8,128)(2,1)}), bf16[32,128,128]{2,1,0:T(8,128)(2,1)S(1)}, u32[]{:S(2)}, u32[]{:S(2)}) async-start(bf16[32,128,128]{2,1,0:T(8,128)(2,1)} %bitcast.16), calls=%async_computation.2 | async-start | bytes 2097152 | tf_op jit(solution)/shard_map/all_to_all | solution.py:116
  105.2 5.8 %copy-start.1 = (f32[512,4096]{1,0:T(8,128)S(1)}, f32[512,4096]{1,0:T(8,128)}, u32[]{:S(2)}) copy-start(f32[512,4096]{1,0:T(8,128)} %get-tuple-element.39) | copy-start | bytes 25165828
  114.0 1.9 copy-start.2
  114.0 27.0 %copy-start.7 = (bf16[1,256,768]{2,1,0:T(8,128)(2,1)S(1)}, bf16[1,256,768]{2,1,0:T(8,128)(2,1)}, u32[]{:S(2)}) copy-start(bf16[1,256,768]{2,1,0:T(8,128)(2,1)} %param.8) | copy-start | bytes 1179652
  114.0 42.8 %copy-start.10 = (bf16[32,16,128]{2,1,0:T(8,128)(2,1)S(1)}, bf16[32,16,128]{2,1,0:T(8,128)(2,1)}, u32[]{:S(2)}) copy-start(bf16[32,16,128]{2,1,0:T(8,128)(2,1)} %copy-done.9) | copy-start | bytes 393220
  117.9 17.8 %all-to-all-start.4 = ((bf16[32,16,128]{2,1,0:T(8,128)(2,1)}), bf16[32,16,128]{2,1,0:T(8,128)(2,1)S(1)}, u32[]{:S(2)}, u32[]{:S(2)}) async-start(bf16[32,16,128]{2,1,0:T(8,128)(2,1)} %convolution_convert_fusion.2), calls=%async_computation.4 | async-start | bytes 262144 | tf_op jit(solution)/shard_map/all_to_all | solution.py:131
  135.7 0.7 copy-start.6
  136.4 26.8 %all-to-all-start.5 = ((bf16[32,128,128]{2,1,0:T(8,128)(2,1)}), bf16[32,128,128]{2,1,0:T(8,128)(2,1)S(1)}, u32[]{:S(2)}, u32[]{:S(2)}) async-start(bf16[32,128,128]{2,1,0:T(8,128)(2,1)} %bitcast.30), calls=%async_computation.5 | async-start | bytes 2097152 | tf_op jit(solution)/shard_map/all_to_all | solution.py:138
  141.0 15.2 %collective-permute-start = (bf16[1,768]{1,0:T(2,128)(2,1)S(1)}, bf16[1,768]{1,0:T(2,128)(2,1)S(1)}, u32[]{:S(2)}, u32[]{:S(2)}) collective-permute-start(bf16[1,768]{1,0:T(2,128)(2,1)S(1)} %slice_bitcast_fusion), channel_id=1, source_target_pairs={{0,16},{16,32},{32,48},{48,64},{64,80},{80,96},{96,112},{112,128},... | collective-permute-start | bytes 4616 | tf_op jit(solution)/shard_map/ppermute | solution.py:16
  163.2 32.3 %all-to-all-start.6 = ((bf16[32,128,128]{2,1,0:T(8,128)(2,1)}), bf16[32,128,128]{2,1,0:T(8,128)(2,1)S(1)}, u32[]{:S(2)}, u32[]{:S(2)}) async-start(bf16[32,128,128]{2,1,0:T(8,128)(2,1)} %bitcast.146), calls=%async_computation.6 | async-start | bytes 2097152 | tf_op jit(solution)/shard_map/all_to_all | solution.py:145
  175.9 248.8 %reduce-scatter.4.cloned.1.call-start = ((), (), s32[]{:S(2)}) async-start(), calls=%async_computation.9 | async-start | bytes 3649536
  198.0 7.9 %copy-start.8 = (bf16[128,768]{1,0:T(8,128)(2,1)}, bf16[128,768]{1,0:T(8,128)(2,1)S(1)}, u32[]{:S(2)}) copy-start(bf16[128,768]{1,0:T(8,128)(2,1)S(1)} %fusion.22) | copy-start | bytes 589828
  205.9 337.1 %all-reduce.2.cloned.1.call-start = ((), (), s32[]{:S(2)}) async-start(), calls=%async_computation.8 | async-start | bytes 221184 | tf_op jit(solution)/shard_map/psum | solution.py:197
Sparse Core Ops, SparseCore 0:
  206.0 218.6 reduce-scatter.3
  427.8 115.2 all-reduce.1
where the time goes:
time: 553 us; the launch traced here: 552 us
  waiting for transfers between devices  412 us (75%)
  starting transfers between devices  55.9 us (10%)
  matrix products  31.5 us (6%)
  local copies, waits for them, and re-layouts  23.9 us (4%)
  between operations  15.1 us (3%)
  other arithmetic  13.3 us (2%)
    unnamed x3, waiting for transfers between devices  219 us
    psum x1, waiting for transfers between devices, on_device(): conv_grad = lax.psum(partial_value, 'dp').astype(jnp.float32)  117 us
    all_to_all x1, waiting for transfers between devices, on_device(): lax.all_to_all(copy_rows(keys_own), 'seq', split_axis=0, concat_axis=0, t...  23.2 us
    all_to_all x1, waiting for transfers between devices, on_device(): lax.all_to_all(copy_rows(values), 'seq', split_axis=0, concat_axis=0, til...  15.8 us
    all_to_all x1, starting transfers between devices, on_device(): lax.all_to_all(grad_value.astype(jnp.bfloat16).reshape(slot_count, tokens...  12.7 us
    unnamed x32, local copies, waits for them, and re-layouts  12.4 us
    ppermute x1, waiting for transfers between devices, passed_along(): return lax.ppermute(value, axis, pairs)  11.8 us
  transfers between devices with their start and end apart: 10, of which 9 were waited for; matrix products, arithmetic and copies ran while one was open for 6% of the time, Pallas kernels for 0%

commit v1 on v0

v1 whole, which is shorter than its diff:
```python
import math

import jax
import jax.numpy as jnp
from jax import lax
from jax.experimental import pallas as pl
from jax.experimental.pallas import tpu as pltpu
from jax.sharding import PartitionSpec as P

EPSILON = 1e-06
LAST_BOTH = (((1,), (1,)), ((), ()))
FIRST_BOTH = (((0,), (0,)), ((), ()))
MESH = pl.DeviceIdType.MESH
BF16, F32 = jnp.bfloat16, jnp.float32

NX, NY, NZ = 4, 8, 8
TOK, CH, HEADS, HS = 128, 768, 4, 128
QROWS = 512
SPAN = CH // (NX * NY)
PAD = 80
HALF = CH // 2


def unit_rows(raw):
    inv = lax.rsqrt(jnp.mean(raw * raw, axis=-1, keepdims=True) + EPSILON)
    return raw * inv, inv


def unit_back(upstream, unit, inv):
    return inv * (upstream - unit * jnp.mean(unit * upstream, axis=-1, keepdims=True))


def kernel(
    rows_ref, feat_ref, gain_ref, wq_ref, wk_ref, wv_ref, temper_ref, hg_ref,
    fg_out, cg_out,
    prev, okv, oqg, kv, qg, raw, wt, wbuf, e_buf, gp_buf, dkv, sib_in, stage, mid_in, end_in, back, total,
    dq_out, dq_back, dall, fgs, fgb, part, yb, tb, zb, fin, fin_sib,
    prev_sem, a_send, a_recv, q_send, q_recv, k_send, k_recv, w_send, w_recv,
    s_send, s_recv, m_send, m_recv, b_send, b_recv, g_send, g_recv, t_send, t_recv, z_send, z_recv, f_send, f_recv, c_sem,
):
    seq, dp = lax.axis_index("seq"), lax.axis_index("dp")
    x, y = lax.div(seq, NY), lax.rem(seq, NY)
    z, core = lax.div(dp, 2), lax.rem(dp, 2)
    n_seq = NX * NY
    xr, xl, xo = lax.rem(x + 1, NX), lax.rem(x + NX - 1, NX), lax.rem(x + 2, NX)
    sib = dp + 1 - 2 * core
    part_y, head = lax.rem(y, 2), lax.div(y, 2)
    me = 2 * x + core

    def at(xx, yy):
        return xx * NY + yy

    def copy(src, dst, send, recv, where):
        return pltpu.make_async_remote_copy(
            src_ref=src, dst_ref=dst, send_sem=send, recv_sem=recv, device_id=where, device_id_type=MESH
        )

    def arrived(dst, recv):
        copy(dst, dst, recv, recv, (seq, sib)).wait_recv()

    def rows_of(ref, start, size):
        return ref.at[pl.ds(pl.multiple_of(start, 16), size)]

    servers = [(at(x, 2 * i + core), 2 * z + 1 - lax.rem(y, 2)) for i in range(HEADS)]
    owners = [(at(x, 2 * j + 1 - core), 2 * z + part_y) for j in range(4)]
    ring_next, ring_prev = (lax.rem(seq + 1, n_seq), dp), (lax.rem(seq + n_seq - 1, n_seq), dp)
    right, left, twin, far = (at(xr, y), dp), (at(xl, y), dp), (seq, sib), (at(xo, y), dp)
    right_twin, left_twin = (at(xr, y), sib), (at(xl, y), sib)
    on_y = [(at(x, lax.rem(y + i, NY)), dp) for i in range(1, NY)]
    on_z = [(seq, lax.rem(dp + 2 * i, 2 * NZ)) for i in range(1, NZ)]

    barrier = pltpu.get_barrier_semaphore()
    partners = servers + owners + [ring_next, ring_prev, right, left, twin, far, right_twin, left_twin] + on_y + on_z
    for where in partners:
        pl.semaphore_signal(barrier, inc=1, device_id=where, device_id_type=MESH)

    feats = feat_ref[...].astype(F32)
    inv_rms = lax.rsqrt(jnp.mean(feats * feats, axis=1, keepdims=True) + EPSILON)
    gain = gain_ref[...]
    normed = (feats * inv_rms * gain).astype(BF16)
    raw[0] = jnp.dot(normed, wq_ref[...], preferred_element_type=F32)
    raw[1] = jnp.dot(normed, wk_ref[...], preferred_element_type=F32)
    values = jnp.dot(normed, wv_ref[...], preferred_element_type=F32).astype(BF16)
    for i in range(HEADS):
        cols = slice(i * HS, (i + 1) * HS)
        okv[i, :, 0:HS] = unit_rows(raw[1, :, cols])[0].astype(BF16)
        okv[i, :, HS:] = values[:, cols]
        oqg[i, :, 0:HS] = unit_rows(raw[0, :, cols])[0].astype(BF16)
        oqg[i, :, HS:] = hg_ref[:, cols]

    pl.semaphore_wait(barrier, len(partners))

    slot = lax.div(y, 2)
    their_me = 2 * x + 1 - lax.rem(y, 2)
    sends = []
    for i in range(HEADS):
        to_kv = kv.at[their_me, pl.ds(pl.multiple_of(slot * TOK, TOK), TOK)]
        sends.append(copy(okv.at[i], to_kv, a_send.at[i], a_recv.at[slot], servers[i]))
    for i in range(HEADS):
        sends.append(copy(oqg.at[i], rows_of(qg, slot * TOK, TOK), q_send.at[i], q_recv.at[slot], servers[i]))
    sends.append(copy(rows_ref.at[pl.ds(2 * TOK - 16, 16)], prev, prev_sem.at[0], prev_sem.at[1], ring_next))
    for one in sends:
        one.start()

    arrived(prev, prev_sem.at[1])
    row = lax.broadcasted_iota(jnp.int32, (2 * TOK, 3 * TOK), 0)
    lane = lax.broadcasted_iota(jnp.int32, (2 * TOK, 3 * TOK), 1)
    chosen = (row == 2 * lax.rem(lane, TOK) + lax.div(lane, TOK) - 1).astype(F32).astype(BF16)
    taps = lax.dot_general(rows_ref[...], chosen, FIRST_BOTH, preferred_element_type=F32)
    row = lax.broadcasted_iota(jnp.int32, (16, TOK), 0)
    lane = lax.broadcasted_iota(jnp.int32, (16, TOK), 1)
    first = ((row == 15) & (lane == 0) & (seq > 0)).astype(F32).astype(BF16)
    tap0 = taps[:, 0:TOK] + lax.dot_general(prev[...], first, FIRST_BOTH, preferred_element_type=F32)
    three = (tap0, taps[:, TOK : 2 * TOK], taps[:, 2 * TOK :])
    zeros = jnp.zeros((PAD - 3 * SPAN, TOK), F32)
    for i in range(NX):
        for j in range(NY):
            low = (i * NY + j) * SPAN
            block = jnp.concatenate([tap[low : low + SPAN] for tap in three] + [zeros], axis=0)
            wt[i, j * PAD : (j + 1) * PAD] = block.astype(BF16)

    def w_slot(xx, cc):
        return wbuf.at[:, pl.ds(pl.multiple_of((2 * xx + cc) * TOK, TOK), TOK)]

    def kv_quarter(block, j):
        return kv.at[block, pl.ds(j * TOK, TOK)]

    def kv_half(block, j):
        return kv.at[block, pl.ds(j * 2 * TOK, 2 * TOK)]

    from_left, from_right, from_far = 2 * xl + core, 2 * xr + core, 2 * xo + core
    for j in range(4):
        arrived(kv_quarter(me, j), a_recv.at[j])
        if j % 2:
            half = j // 2
            for i, (where, slot_at) in enumerate(((right, half), (left, 2 + half), (twin, 6 + half))):
                one = copy(kv_half(me, half), kv_half(me, half), k_send.at[3 * half + i], k_recv.at[slot_at], where)
                one.start()
                sends.append(one)
    for i, (block, slot_at, take, onward, far_at) in enumerate(
        ((from_left, 0, 0, right, 4), (from_right, 2, 1, left, 5))
    ):
        for half in range(2):
            arrived(kv_half(block, half), k_recv.at[slot_at + half])
            if half == take:
                one = copy(kv_half(block, half), kv_half(block, half), k_send.at[6 + i], k_recv.at[far_at], onward)
                one.start()
                sends.append(one)
        one = copy(kv.at[block], kv.at[block], k_send.at[8 + i], k_recv.at[8 + i], twin)
        one.start()
        sends.append(one)

    wbuf[:, pl.ds(pl.multiple_of(me * TOK, TOK), TOK)] = wt[x]
    for i, where in enumerate((right, left, far)):
        to_x = (xr, xl, xo)[i]
        one = copy(wt.at[to_x], w_slot(x, core), w_send.at[i], w_recv.at[i], where)
        one.start()
        sends.append(one)
    one = copy(wt.at[x], w_slot(x, core), w_send.at[3], w_recv.at[3], twin)
    one.start()
    sends.append(one)

    for j in range(4):
        arrived(rows_of(qg, j * TOK, TOK), q_recv.at[j])
    factor = temper_ref[head] * (1.0 / math.sqrt(HS))
    queries, upstream = qg[:, 0:HS], qg[:, HS:]

    def first_pass(block, sums):
        scores = lax.dot_general(kv[block, :, 0:HS], queries, LAST_BOTH, preferred_element_type=F32)
        expo = jnp.exp2(scores * (factor * math.log2(math.e)))
        e_buf[block] = expo
        grad_prob = lax.dot_general(kv[block, :, HS:], upstream, LAST_BOTH, preferred_element_type=F32)
        gp_buf[block] = grad_prob
        return (
            sums[0] + jnp.sum(expo, axis=0, keepdims=True),
            sums[1] + jnp.sum(expo * grad_prob, axis=0, keepdims=True),
        )

    sums = (jnp.zeros((1, QROWS), F32), jnp.zeros((1, QROWS), F32))
    sums = first_pass(me, sums)
    for half in range(2):
        arrived(kv_half(me + 1 - 2 * core, half), k_recv.at[6 + half])
    sums = first_pass(me + 1 - 2 * core, sums)
    sums = first_pass(from_left, sums)
    sums = first_pass(from_right, sums)
    arrived(kv_half(from_far, 0), k_recv.at[4])
    arrived(kv_half(from_far, 1), k_recv.at[5])
    one = copy(kv.at[from_far], kv.at[from_far], k_send.at[10], k_recv.at[10], twin)
    one.start()
    sends.append(one)
    for i, other in enumerate((2 * xl + 1 - core, 2 * xr + 1 - core)):
        arrived(kv.at[other], k_recv.at[8 + i])
        sums = first_pass(other, sums)
    sums = first_pass(from_far, sums)
    far_other = 2 * xo + 1 - core
    arrived(kv.at[far_other], k_recv.at[10])
    sums = first_pass(far_other, sums)

    for i, from_x in enumerate((xl, xr, xo)):
        arrived(w_slot(from_x, core), w_recv.at[i])
        one = copy(w_slot(from_x, core), w_slot(from_x, core), w_send.at[4 + i], w_recv.at[4 + i], twin)
        one.start()
        sends.append(one)

    inv_sum = 1.0 / sums[0]
    grad_dot = sums[1] * inv_sum

    def second_pass(block, grad_query):
        prob = e_buf[block] * inv_sum
        grad_score = (prob * ((gp_buf[block] - grad_dot) * factor)).astype(BF16)
        dkv[block, :, HS:] = jnp.dot(prob.astype(BF16), upstream, preferred_element_type=F32).astype(BF16)
        dkv[block, :, 0:HS] = jnp.dot(grad_score, queries, preferred_element_type=F32).astype(BF16)
        keys_t = jnp.transpose(kv[block, :, 0:HS])
        return grad_query + jnp.dot(keys_t, grad_score, preferred_element_type=F32)

    grad_query = jnp.zeros((HS, QROWS), F32)
    half_rows = QROWS // 2
    for i, to_x in enumerate((xo, xr, xl, x)):
        grad_query = second_pass(2 * to_x + 1 - core, grad_query)
        one = copy(dkv.at[2 * to_x + 1 - core], sib_in.at[i], s_send.at[i], s_recv.at[i], twin)
        one.start()
        sends.append(one)
        grad_query = second_pass(2 * to_x + core, grad_query)
        if i == 3:
            dq_out[...] = jnp.transpose(grad_query).astype(BF16)
            for j in range(4):
                one = copy(
                    dq_out.at[pl.ds(j * TOK, TOK)], dq_back.at[head], b_send.at[j], b_recv.at[head], owners[j]
                )
                one.start()
                sends.append(one)
        arrived(sib_in.at[i], s_recv.at[i])
        summed = dkv[2 * to_x + core].astype(F32) + sib_in[i].astype(F32)
        if i == 0:
            stage[0] = summed.astype(BF16)
            for k, where in enumerate((right, left)):
                src = stage.at[0, pl.ds(k * half_rows, half_rows)]
                one = copy(src, mid_in.at[k], m_send.at[k], m_recv.at[k], where)
                one.start()
                sends.append(one)
        elif i < 3:
            k = i - 1
            arrived(mid_in.at[k], m_recv.at[k])
            both = (summed[0:half_rows], summed[half_rows:])
            mine = both[k] + mid_in[k].astype(F32)
            stage[i, k * half_rows : (k + 1) * half_rows] = mine.astype(BF16)
            stage[i, (1 - k) * half_rows : (2 - k) * half_rows] = both[1 - k].astype(BF16)
            one = copy(stage.at[i], end_in.at[k], m_send.at[2 + k], m_recv.at[2 + k], (right, left)[k])
            one.start()
            sends.append(one)
        else:
            for k in range(2):
                arrived(end_in.at[k], m_recv.at[2 + k])
            total[...] = (summed + end_in[0].astype(F32) + end_in[1].astype(F32)).astype(BF16)
            for j in range(4):
                src = total.at[pl.ds(j * TOK, TOK)]
                one = copy(src, back.at[head], b_send.at[4 + j], b_recv.at[4 + head], owners[j])
                one.start()
                sends.append(one)

    def put_raw_grad(which, i, upstream_grad):
        unit, inv = unit_rows(raw[which, :, i * HS : (i + 1) * HS])
        dall[which, :, i * HS : (i + 1) * HS] = unit_back(upstream_grad.astype(F32), unit, inv).astype(BF16)

    for i in range(HEADS):
        arrived(dq_back.at[i], b_recv.at[i])
        put_raw_grad(0, i, dq_back[i])
    grad_normed = lax.dot_general(dall[0], wq_ref[...], LAST_BOTH, preferred_element_type=F32)
    for i in range(HEADS):
        arrived(back.at[i], b_recv.at[4 + i])
        put_raw_grad(1, i, back[i, :, 0:HS])
        dall[2, :, i * HS : (i + 1) * HS] = back[i, :, HS:]
    grad_normed += lax.dot_general(dall[1], wk_ref[...], LAST_BOTH, preferred_element_type=F32)
    grad_normed += lax.dot_general(dall[2], wv_ref[...], LAST_BOTH, preferred_element_type=F32)
    gained = grad_normed * gain
    unit_feats = feats * inv_rms
    feature_grad = inv_rms * (gained - unit_feats * jnp.mean(unit_feats * gained, axis=1, keepdims=True))
    feature_grad = feature_grad.astype(BF16)
    fg_out[...] = feature_grad
    fgs[0] = feature_grad[:, 0:HALF]
    fgs[1] = feature_grad[:, HALF:]

    def g_slot(xx, cc):
        return rows_of(fgb, (2 * xx + cc) * TOK, TOK)

    fgb[pl.ds(pl.multiple_of(me * TOK, TOK), TOK)] = fgs[core]
    for i, (where, cc, slot_at) in enumerate(
        (
            (right, core, core),
            (left, core, 2 + core),
            (right_twin, 1 - core, core),
            (left_twin, 1 - core, 2 + core),
            (twin, 1 - core, 6),
        )
    ):
        one = copy(fgs.at[cc], g_slot(x, core), g_send.at[i], g_recv.at[slot_at], where)
        one.start()
        sends.append(one)
    arrived(g_slot(xl, 0), g_recv.at[0])
    one = copy(g_slot(xl, 0), g_slot(xl, 0), g_send.at[5], g_recv.at[4], right)
    one.start()
    sends.append(one)
    arrived(g_slot(xr, 1), g_recv.at[3])
    one = copy(g_slot(xr, 1), g_slot(xr, 1), g_send.at[6], g_recv.at[5], left)
    one.start()
    sends.append(one)
    for i, from_x in enumerate((xl, xr, xo)):
        arrived(w_slot(from_x, 1 - core), w_recv.at[4 + i])
    arrived(w_slot(x, 1 - core), w_recv.at[3])
    arrived(g_slot(xl, 1), g_recv.at[1])
    arrived(g_slot(xr, 0), g_recv.at[2])
    arrived(g_slot(x, 1 - core), g_recv.at[6])
    arrived(g_slot(xo, 0), g_recv.at[4])
    arrived(g_slot(xo, 1), g_recv.at[5])
    part[...] = (jnp.dot(wbuf[...], fgb[...], preferred_element_type=F32) * (1.0 / (2 * NZ))).astype(BF16)

    yb[y] = part[pl.ds(pl.multiple_of(y * PAD, 16), PAD)]
    for i in range(1, NY):
        to_y = lax.rem(y + i, NY)
        one = copy(rows_of(part, to_y * PAD, PAD), yb.at[y], t_send.at[i - 1], t_recv.at[y], on_y[i - 1])
        one.start()
        sends.append(one)
    for i in range(1, NY):
        from_y = lax.rem(y + i, NY)
        arrived(yb.at[from_y], t_recv.at[from_y])
    block = yb[0].astype(F32)
    for i in range(1, NY):
        block += yb[i].astype(F32)

    for i in range(PAD // 16):
        for j in range(HALF // 128):
            tb[3 * i + j] = block[16 * i : 16 * (i + 1), 128 * j : 128 * (j + 1)].astype(BF16)
    tb[15] = jnp.zeros((16, 128), BF16)
    zb[z] = tb[pl.ds(2 * z, 2)]
    for i in range(1, NZ):
        to_z = lax.rem(z + i, NZ)
        one = copy(tb.at[pl.ds(2 * to_z, 2)], zb.at[z], z_send.at[i - 1], z_recv.at[z], on_z[i - 1])
        one.start()
        sends.append(one)
    for i in range(1, NZ):
        from_z = lax.rem(z + i, NZ)
        arrived(zb.at[from_z], z_recv.at[from_z])
    tiles = zb[0].astype(F32)
    for i in range(1, NZ):
        tiles += zb[i].astype(F32)
    fin[pl.ds(2 * z, 2)] = tiles
    for i in range(1, NZ):
        mine = fin.at[pl.ds(2 * z, 2)]
        one = copy(mine, mine, f_send.at[i - 1], f_recv.at[z], on_z[i - 1])
        one.start()
        sends.append(one)
    for i in range(1, NZ):
        from_z = lax.rem(z + i, NZ)
        arrived(fin.at[pl.ds(2 * from_z, 2)], f_recv.at[from_z])
    one = copy(fin, fin_sib, c_sem.at[0], c_sem.at[1], twin)
    one.start()
    sends.append(one)
    arrived(fin_sib, c_sem.at[1])
    own, other = fin[...], fin_sib[...]
    for half in range(2):
        mine = jnp.where(core == half, own, other)
        wide = [jnp.concatenate([mine[3 * i + j] for j in range(3)], axis=1) for i in range(PAD // 16)]
        wide = jnp.concatenate(wide, axis=0)
        for k in range(3):
            cg_out[k, :, half * HALF : (half + 1) * HALF] = wide[k * SPAN : (k + 1) * SPAN]

    for one in sends:
        one.wait_send()


def on_device(input_rows, features, norm_gain, w_query, w_key, w_value, temper, head_grads):
    vmem = pl.BlockSpec(memory_space=pltpu.VMEM)
    dma = pltpu.SemaphoreType.DMA

    def scratch(*shape, dtype=BF16):
        return pltpu.VMEM(shape, dtype)

    fg, cg = pl.pallas_call(
        kernel,
        out_shape=(
            jax.ShapeDtypeStruct((TOK, CH), BF16),
            jax.ShapeDtypeStruct((3, SPAN, CH), F32),
        ),
        in_specs=[vmem] * 6 + [pl.BlockSpec(memory_space=pltpu.SMEM), vmem],
        out_specs=(vmem, vmem),
        scratch_shapes=[
            scratch(16, CH),
            scratch(HEADS, TOK, 2 * HS),
            scratch(HEADS, TOK, 2 * HS),
            scratch(8, QROWS, 2 * HS),
            scratch(QROWS, 2 * HS),
            scratch(2, TOK, HEADS * HS, dtype=F32),
            scratch(NX, NY * PAD, TOK),
            scratch(NY * PAD, 8 * TOK),
            scratch(8, QROWS, QROWS, dtype=F32),
            scratch(8, QROWS, QROWS, dtype=F32),
            scratch(8, QROWS, 2 * HS),
            scratch(NX, QROWS, 2 * HS),
            scratch(3, QROWS, 2 * HS),
            scratch(2, QROWS // 2, 2 * HS),
            scratch(2, QROWS, 2 * HS),
            scratch(HEADS, TOK, 2 * HS),
            scratch(QROWS, 2 * HS),
            scratch(QROWS, HS),
            scratch(HEADS, TOK, HS),
            scratch(3, TOK, HEADS * HS),
            scratch(2, TOK, HALF),
            scratch(8 * TOK, HALF),
            scratch(NY * PAD, HALF),
            scratch(NY, PAD, HALF),
            scratch(16, 16, 128),
            scratch(NZ, 2, 16, 128),
            scratch(16, 16, 128, dtype=F32),
            scratch(16, 16, 128, dtype=F32),
            dma((2,)),
            dma((4,)), dma((4,)),
            dma((4,)), dma((4,)),
            dma((11,)), dma((11,)),
            dma((7,)), dma((7,)),
            dma((4,)), dma((4,)),
            dma((4,)), dma((4,)),
            dma((8,)), dma((8,)),
            dma((7,)), dma((7,)),
            dma((7,)), dma((8,)),
            dma((7,)), dma((8,)),
            dma((7,)), dma((8,)),
            dma((2,)),
        ],
        compiler_params=pltpu.CompilerParams(
            collective_id=0, has_side_effects=True, vmem_limit_bytes=56 * 1024 * 1024
        ),
    )(
        input_rows[0], features[0], norm_gain.reshape(1, CH), w_query, w_key, w_value, temper, head_grads[0],
    )
    return fg[None], cg


def solution(mesh):
    return jax.shard_map(
        on_device,
        mesh=mesh,
        in_specs=(
            P("dp", "seq", None),
            P("dp", "seq", None),
            P(),
            P(),
            P(),
            P(),
            P(),
            P("dp", "seq", None),
        ),
        out_specs=(P("dp", "seq", None), P(None, "seq", None)),
        check_vma=False,
    )
```

time: 553 us -> 120 us (0.22)
  waiting for transfers between devices: 412 us -> 0 us
  Pallas kernels: 0 us -> 115 us
  starting transfers between devices: 55.9 us -> 0 us
  matrix products: 31.5 us -> 0 us
  local copies, waits for them, and re-layouts: 23.9 us -> 3.61 us
  between operations: 15.1 us -> 0.66 us
  other arithmetic: 13.3 us -> 0 us
    unnamed x3 -> x0, waiting for transfers between devices: 219 us -> none
    psum x1 -> x0, waiting for transfers between devices: 117 us -> none  [on_device(): conv_grad = lax.psum(partial_value, 'dp').astype(jnp.float32)]
    pallas_call x0 -> x1, Pallas kernels: none -> 115 us  [on_device(): pl.pallas_call(kernel, out_shape=(jax.ShapeDtypeStruct((TOK, CH), BF16),...]
    all_to_all x7 -> x0, waiting for transfers between devices: 64.5 us -> none  [the longest x1 23.2 us: on_device(): lax.all_to_all(copy_rows(keys_own), 'seq', split_axis=0, concat_axis=0, t...]
    all_to_all x7 -> x0, starting transfers between devices: 52.5 us -> none  [the longest x1 12.7 us: on_device(): lax.all_to_all(grad_value.astype(jnp.bfloat16).reshape(slot_count, tokens...]
    dot_general x12 -> x0, matrix products: 31.5 us -> none  [the longest x1 6.35 us: one_block(): lax.dot_general(prob_low, upstream_rows, FIRST_BOTH, preferred_element_ty...]
    ppermute x1 -> x0, waiting for transfers between devices: 11.8 us -> none  [passed_along(): return lax.ppermute(value, axis, pairs)]
    unnamed x32 -> x6, local copies, waits for them, and re-layouts: 12.4 us -> 3.03 us
  transfers between devices with their start and end apart: 10 -> 0, of which waited for: 9 -> 0; matrix products, arithmetic and copies ran while one was open for 6% -> 0% of each run, Pallas kernels for 0% -> 0%
where the time goes in v1:
time: 120 us; the launch traced here: 119 us
  Pallas kernels  115 us (96%)
  local copies, waits for them, and re-layouts  3.61 us (3%)
    pallas_call x1, Pallas kernels, on_device(): pl.pallas_call(kernel, out_shape=(jax.ShapeDtypeStruct((TOK, CH), BF16),...  115 us
    unnamed x6, local copies, waits for them, and re-layouts  3.03 us

profile of v1, /device:TPU:1, one launch (start us, length us, event | category | flops | bytes accessed | tf_op | source)
XLA Modules:
  0.0 119.4 jit_solution(1967803454039115069)
XLA Ops:
  0.6 0.0 copy-start.1
  0.6 0.7 copy-done.1
  1.3 0.6 reshape.7.gain_ref
  1.9 115.2 %shard_map.95 = (bf16[128,768]{1,0:T(8,128)(2,1)}, f32[3,24,768]{2,1,0:T(8,128)}) custom-call(bf16[256,768]{1,0:T(8,128)(2,1)} %bitcast.4, bf16[128,768]{1,0:T(8,128)(2,1)} %bitcast.6, f32[1,768]{1,0:T(1,128)} %reshape.7.gain_ref, bf16[768,512]{1,0:T(8,128)(2,1)} %wq_ref.1, bf16[768,512]{1,0:T(8,128)(2,1)} %wk_ref.1, bf16[768,512]{1,0:T(8,128)(2,1)} %wv_ref.1, ...), custom_call_target="tpu_custom_call" | custom-call | tf_op jit(solution)/shard_map/pallas_call | solution.py:378
  117.1 0.0 copy-start
  117.1 1.7 %copy.12 = bf16[1,128,768]{2,1,0:T(8,128)(2,1)} copy(bf16[1,128,768]{2,1,0:T(8,128)(2,1)} %bitcast.5) | data formatting | bytes 393216
  118.7 0.0 copy-done
  118.7 0.7 copy.13
Async XLA Ops:
  0.6 0.7 copy-start.1
  117.1 1.7 %copy-start = (f32[3,24,768]{2,1,0:T(8,128)S(1)}, f32[3,24,768]{2,1,0:T(8,128)}, u32[]{:S(2)}) copy-start(f32[3,24,768]{2,1,0:T(8,128)} %get-tuple-element.9) | copy-start | bytes 663556

commit v2 on v1

v2 whole, which is shorter than its diff:
```python
import math

import jax
import jax.numpy as jnp
from jax import lax
from jax.experimental import pallas as pl
from jax.experimental.pallas import tpu as pltpu
from jax.sharding import PartitionSpec as P

EPSILON = 1e-06
LAST_BOTH = (((1,), (1,)), ((), ()))
FIRST_BOTH = (((0,), (0,)), ((), ()))
MESH = pl.DeviceIdType.MESH
BF16, F32 = jnp.bfloat16, jnp.float32

NX, NY, NZ = 4, 8, 8
TOK, CH, HEADS, HS = 128, 768, 4, 128
QROWS = 512
SPAN = CH // (NX * NY)
PAD = 80
HALF = CH // 2


def unit_rows(raw):
    inv = lax.rsqrt(jnp.mean(raw * raw, axis=-1, keepdims=True) + EPSILON)
    return raw * inv, inv


def unit_back(upstream, unit, inv):
    return inv * (upstream - unit * jnp.mean(unit * upstream, axis=-1, keepdims=True))


def kernel(
    rows_ref, feat_ref, gain_ref, wq_ref, wk_ref, wv_ref, temper_ref, hg_ref,
    fg_out, cg_out,
    prev, outgoing, keys, vals, qg, raw, wt, wbuf, e_buf, gp_buf, dv, dk, sib_v, sib_k, st_v, st_k, in_v, in_k,
    total, back, dall, fgs, fgb, part, yb1, zb1, s1, s2, zb2, yb2, fin, fin_sib,
    prev_sem, a_send, a_recv, k_send, k_recv, w_send, w_recv, sv_send, sv_recv, sk_send, sk_recv,
    mv_send, mv_recv, mk_send, mk_recv, b_send, b_recv, g_send, g_recv, t_send, t_recv, u_send, u_recv, f_send, f_recv, c_sem,
):
    seq, dp = lax.axis_index("seq"), lax.axis_index("dp")
    x, y = lax.div(seq, NY), lax.rem(seq, NY)
    z, core = lax.div(dp, 2), lax.rem(dp, 2)
    n_seq = NX * NY
    xr, xl, xo = lax.rem(x + 1, NX), lax.rem(x + NX - 1, NX), lax.rem(x + 2, NX)
    sib = dp + 1 - 2 * core
    part_y, head = lax.rem(y, 2), lax.div(y, 2)
    me = 2 * x + core

    def at(xx, yy):
        return xx * NY + yy

    def copy(src, dst, send, recv, where):
        return pltpu.make_async_remote_copy(
            src_ref=src, dst_ref=dst, send_sem=send, recv_sem=recv, device_id=where, device_id_type=MESH
        )

    sends = []

    def send(src, dst, send_sem, recv_sem, where):
        one = copy(src, dst, send_sem, recv_sem, where)
        one.start()
        sends.append(one)
        return one

    def arrived(dst, recv):
        copy(dst, dst, recv, recv, (seq, sib)).wait_recv()

    def rows_of(ref, start, size):
        return ref.at[pl.ds(pl.multiple_of(start, 16), size)]

    servers = [(at(x, 2 * i + core), 2 * z + 1 - lax.rem(y, 2)) for i in range(HEADS)]
    owners = [(at(x, 2 * j + 1 - core), 2 * z + part_y) for j in range(4)]
    ring_next, ring_prev = (lax.rem(seq + 1, n_seq), dp), (lax.rem(seq + n_seq - 1, n_seq), dp)
    right, left, twin, far = (at(xr, y), dp), (at(xl, y), dp), (seq, sib), (at(xo, y), dp)
    right_twin, left_twin = (at(xr, y), sib), (at(xl, y), sib)
    on_y = [(at(x, lax.rem(y + i, NY)), dp) for i in range(1, NY)]
    on_z = [(seq, lax.rem(dp + 2 * i, 2 * NZ)) for i in range(1, NZ)]

    barrier = pltpu.get_barrier_semaphore()
    partners = servers + owners + [ring_next, ring_prev, right, left, twin, far, right_twin, left_twin] + on_y + on_z
    for where in partners:
        pl.semaphore_signal(barrier, inc=1, device_id=where, device_id_type=MESH)

    feats = feat_ref[...].astype(F32)
    inv_rms = lax.rsqrt(jnp.mean(feats * feats, axis=1, keepdims=True) + EPSILON)
    gain = gain_ref[...]
    normed = (feats * inv_rms * gain).astype(BF16)
    slot = lax.div(y, 2)
    their_me = 2 * x + 1 - lax.rem(y, 2)

    def start_heads(kind, to):
        started = []
        for i in range(HEADS):
            started.append(copy(outgoing.at[kind, i], to, a_send.at[kind, i], a_recv.at[kind, slot], servers[i]))
            started[i].start()
        return started

    def wait_heads(started):
        for one in started:
            one.wait_send()

    def project(which, w_ref):
        raw[which] = jnp.dot(normed, w_ref[...], preferred_element_type=F32)
        for i in range(HEADS):
            outgoing[which, i] = unit_rows(raw[which, :, i * HS : (i + 1) * HS])[0].astype(BF16)

    project(0, wk_ref)
    pl.semaphore_wait(barrier, len(partners))
    slot_rows = pl.ds(pl.multiple_of(slot * TOK, TOK), TOK)
    sent = start_heads(0, keys.at[their_me, slot_rows])
    send(rows_ref.at[pl.ds(2 * TOK - 16, 16)], prev, prev_sem.at[0], prev_sem.at[1], ring_next)
    project(1, wq_ref)
    values = jnp.dot(normed, wv_ref[...], preferred_element_type=F32).astype(BF16)
    for i in range(HEADS):
        outgoing[2, i] = values[:, i * HS : (i + 1) * HS]
        outgoing[3, i] = hg_ref[:, i * HS : (i + 1) * HS]
    wait_heads(sent)
    sent = start_heads(1, qg.at[0, slot_rows])

    arrived(prev, prev_sem.at[1])
    row = lax.broadcasted_iota(jnp.int32, (2 * TOK, 3 * TOK), 0)
    lane = lax.broadcasted_iota(jnp.int32, (2 * TOK, 3 * TOK), 1)
    chosen = (row == 2 * lax.rem(lane, TOK) + lax.div(lane, TOK) - 1).astype(F32).astype(BF16)
    taps = lax.dot_general(rows_ref[...], chosen, FIRST_BOTH, preferred_element_type=F32)
    row = lax.broadcasted_iota(jnp.int32, (16, TOK), 0)
    lane = lax.broadcasted_iota(jnp.int32, (16, TOK), 1)
    first = ((row == 15) & (lane == 0) & (seq > 0)).astype(F32).astype(BF16)
    tap0 = taps[:, 0:TOK] + lax.dot_general(prev[...], first, FIRST_BOTH, preferred_element_type=F32)
    three = (tap0, taps[:, TOK : 2 * TOK], taps[:, 2 * TOK :])
    zeros = jnp.zeros((PAD - 3 * SPAN, TOK), F32)
    for i in range(NX):
        for j in range(NY):
            low = (i * NY + j) * SPAN
            block = jnp.concatenate([tap[low : low + SPAN] for tap in three] + [zeros], axis=0)
            wt[i, j * PAD : (j + 1) * PAD] = block.astype(BF16)

    def chunk(ref, block, i):
        j = lax.rem(slot + (0, 1, 3, 2)[i], 4)
        return ref.at[block, pl.ds(pl.multiple_of(j * TOK, TOK), TOK)], j

    from_left, from_right, from_far = 2 * xl + core, 2 * xr + core, 2 * xo + core
    twin_me, twin_left, twin_right, twin_far = me + 1 - 2 * core, 2 * xl + 1 - core, 2 * xr + 1 - core, 2 * xo + 1 - core
    both = (keys, vals)

    def ring_own(t, i):
        mine, j = chunk(both[t], me, i)
        arrived(mine, a_recv.at[2 * t, j])
        for k, where in enumerate((right, left, twin)):
            send(mine, mine, k_send.at[t, 3 * i + k], k_recv.at[t, (0, 4, 12)[k] + i], where)

    def ring_on(t):
        for i, block, first_slot, onward in (
            (0, from_left, 0, right), (1, from_left, 0, right), (0, from_right, 4, None), (1, from_right, 4, None),
            (2, from_right, 4, left), (3, from_right, 4, left), (2, from_left, 0, None), (3, from_left, 0, None),
        ):
            piece, _ = chunk(both[t], block, i)
            arrived(piece, k_recv.at[t, first_slot + i])
            if onward is not None:
                send(piece, piece, k_send.at[t, 12 + i], k_recv.at[t, 8 + i], onward)
        for k, block in enumerate((from_left, from_right)):
            send(both[t].at[block], both[t].at[block], k_send.at[t, 16 + k], k_recv.at[t, 16 + k], twin)

    def ring_far(t):
        for i in range(4):
            arrived(chunk(both[t], from_far, i)[0], k_recv.at[t, 8 + i])
        send(both[t].at[from_far], both[t].at[from_far], k_send.at[t, 18], k_recv.at[t, 18], twin)

    def got_twin(t):
        for i in range(4):
            arrived(chunk(both[t], twin_me, i)[0], k_recv.at[t, 12 + i])

    def got_from_twin(t, k):
        arrived(both[t].at[(twin_left, twin_right, twin_far)[k]], k_recv.at[t, 16 + k])

    ring_own(0, 0)
    ring_own(0, 1)
    wait_heads(sent)
    sent = start_heads(2, vals.at[their_me, slot_rows])
    ring_own(0, 2)
    ring_own(0, 3)
    wait_heads(sent)
    sends += start_heads(3, qg.at[1, slot_rows])
    ring_on(0)

    for j in range(4):
        arrived(qg.at[0, pl.ds(j * TOK, TOK)], a_recv.at[1, j])
    factor = temper_ref[head] * (1.0 / math.sqrt(HS))

    def score_pass(block, exp_sum):
        scores = lax.dot_general(keys[block], qg[0], LAST_BOTH, preferred_element_type=F32)
        expo = jnp.exp2(scores * (factor * math.log2(math.e)))
        e_buf[block] = expo
        return exp_sum + jnp.sum(expo, axis=0, keepdims=True)

    exp_sum = score_pass(me, jnp.zeros((1, QROWS), F32))
    ring_own(1, 0)
    got_twin(0)
    exp_sum = score_pass(twin_me, exp_sum)
    ring_own(1, 1)
    exp_sum = score_pass(from_left, exp_sum)
    ring_own(1, 2)
    exp_sum = score_pass(from_right, exp_sum)
    ring_own(1, 3)
    ring_far(0)
    got_from_twin(0, 0)
    exp_sum = score_pass(twin_left, exp_sum)
    got_from_twin(0, 1)
    exp_sum = score_pass(twin_right, exp_sum)
    ring_on(1)
    exp_sum = score_pass(from_far, exp_sum)
    got_from_twin(0, 2)
    exp_sum = score_pass(twin_far, exp_sum)
    inv_sum = 1.0 / exp_sum

    for j in range(4):
        arrived(qg.at[1, pl.ds(j * TOK, TOK)], a_recv.at[3, j])
    order = (xo, xr, xl, x)
    to = (far, right, left)

    def value_grad(block):
        prob = (e_buf[block] * inv_sum).astype(BF16)
        dv[block] = jnp.dot(prob, qg[1], preferred_element_type=F32).astype(BF16)

    def prob_grad(block, dot_sum):
        grad_prob = lax.dot_general(vals[block], qg[1], LAST_BOTH, preferred_element_type=F32)
        gp_buf[block] = grad_prob
        return dot_sum + jnp.sum(e_buf[block] * grad_prob, axis=0, keepdims=True)

    def pass_values(i):
        arrived(sib_v.at[i], sv_recv.at[i])
        st_v[i] = (dv[2 * order[i] + core].astype(F32) + sib_v[i].astype(F32)).astype(BF16)
        send(st_v.at[i], in_v.at[i], mv_send.at[i], mv_recv.at[i], to[i])

    dot_sum = jnp.zeros((1, QROWS), F32)
    for i in range(NX):
        block = 2 * order[i] + 1 - core
        value_grad(block)
        send(dv.at[block], sib_v.at[i], sv_send.at[i], sv_recv.at[i], twin)
        value_grad(2 * order[i] + core)
        if i > 0:
            pass_values(i - 1)
        if i == 0:
            dot_sum = prob_grad(me, dot_sum)
            got_twin(1)
            dot_sum = prob_grad(twin_me, dot_sum)
        elif i == 1:
            dot_sum = prob_grad(from_left, dot_sum)
            dot_sum = prob_grad(from_right, dot_sum)
            ring_far(1)
        elif i == 2:
            for k, other in enumerate((twin_left, twin_right)):
                got_from_twin(1, k)
                dot_sum = prob_grad(other, dot_sum)
        else:
            dot_sum = prob_grad(from_far, dot_sum)
            got_from_twin(1, 2)
            dot_sum = prob_grad(twin_far, dot_sum)

    grad_dot = dot_sum * inv_sum
    inv_factor = inv_sum * factor
    half_rows = QROWS // 2

    def key_grad(block, half, grad_query):
        low = half * half_rows
        high = low + half_rows
        grad_score = (e_buf[block, low:high] * inv_factor * (gp_buf[block, low:high] - grad_dot)).astype(BF16)
        dk[block, low:high] = jnp.dot(grad_score, qg[0], preferred_element_type=F32).astype(BF16)
        keys_t = jnp.transpose(keys[block, low:high])
        return grad_query + jnp.dot(keys_t, grad_score, preferred_element_type=F32)

    def half_of(ref, i, half):
        return ref.at[i, pl.ds(half * half_rows, half_rows)]

    def pass_keys(half, i):
        low = half * half_rows
        high = low + half_rows
        arrived(half_of(sib_k, i, half), sk_recv.at[half, i])
        summed = dk[2 * order[i] + core, low:high].astype(F32) + sib_k[i, low:high].astype(F32)
        if i < 3:
            st_k[i, low:high] = summed.astype(BF16)
            send(half_of(st_k, i, half), half_of(in_k, i, half), mk_send.at[half, i], mk_recv.at[half, i], to[i])
        return summed

    grad_query = jnp.zeros((HS, QROWS), F32)
    pending = None
    for half in range(2):
        for i in range(NX):
            block = 2 * order[i] + 1 - core
            grad_query = key_grad(block, half, grad_query)
            send(half_of(dk, block, half), half_of(sib_k, i, half), sk_send.at[half, i], sk_recv.at[half, i], twin)
            grad_query = key_grad(2 * order[i] + core, half, grad_query)
            if pending is not None and pending[1] < 3:
                pass_keys(*pending)
            pending = (half, i)
    total[0] = jnp.transpose(grad_query).astype(BF16)

    def start_back(kind, j):
        src = total.at[kind, pl.ds(j * TOK, TOK)]
        send(src, back.at[kind, head], b_send.at[kind, j], b_recv.at[kind, head], owners[j])

    for j in range(4):
        start_back(0, j)
    arrived(sib_v.at[3], sv_recv.at[3])
    summed = dv[me].astype(F32) + sib_v[3].astype(F32)
    for i in range(3):
        arrived(in_v.at[i], mv_recv.at[i])
        summed += in_v[i].astype(F32)
    total[2] = summed.astype(BF16)
    for j in range(4):
        start_back(2, j)
    for half in range(2):
        low = half * half_rows
        high = low + half_rows
        summed = pass_keys(half, 3)
        for i in range(3):
            arrived(half_of(in_k, i, half), mk_recv.at[half, i])
            summed += in_k[i, low:high].astype(F32)
        total[1, low:high] = summed.astype(BF16)
        for j in range(2 * half, 2 * half + 2):
            start_back(1, j)

    def w_slot(xx, cc):
        return wbuf.at[:, pl.ds(pl.multiple_of((2 * xx + cc) * TOK, TOK), TOK)]

    for i, where in enumerate((right, left, far)):
        send(wt.at[(xr, xl, xo)[i]], w_slot(x, core), w_send.at[i], w_recv.at[i], where)
    send(wt.at[x], w_slot(x, core), w_send.at[3], w_recv.at[3], twin)
    wbuf[:, pl.ds(pl.multiple_of(me * TOK, TOK), TOK)] = wt[x]

    def put_raw_grad(which, i, upstream_grad):
        unit, inv = unit_rows(raw[1 - which, :, i * HS : (i + 1) * HS])
        dall[which, :, i * HS : (i + 1) * HS] = unit_back(upstream_grad.astype(F32), unit, inv).astype(BF16)

    for i in range(HEADS):
        arrived(back.at[0, i], b_recv.at[0, i])
        put_raw_grad(0, i, back[0, i])
    grad_normed = lax.dot_general(dall[0], wq_ref[...], LAST_BOTH, preferred_element_type=F32)
    for i in range(HEADS):
        arrived(back.at[2, i], b_recv.at[2, i])
        dall[2, :, i * HS : (i + 1) * HS] = back[2, i]
    grad_normed += lax.dot_general(dall[2], wv_ref[...], LAST_BOTH, preferred_element_type=F32)
    for i in range(HEADS):
        arrived(back.at[1, i], b_recv.at[1, i])
        put_raw_grad(1, i, back[1, i])
    grad_normed += lax.dot_general(dall[1], wk_ref[...], LAST_BOTH, preferred_element_type=F32)
    gained = grad_normed * gain
    unit_feats = feats * inv_rms
    feature_grad = inv_rms * (gained - unit_feats * jnp.mean(unit_feats * gained, axis=1, keepdims=True))
    feature_grad = feature_grad.astype(BF16)
    fg_out[...] = feature_grad
    fgs[0] = feature_grad[:, 0:HALF]
    fgs[1] = feature_grad[:, HALF:]

    def g_slot(xx, cc):
        return rows_of(fgb, (2 * xx + cc) * TOK, TOK)

    for i, (where, cc, slot_at) in enumerate(
        (
            (right, core, core),
            (left, core, 2 + core),
            (right_twin, 1 - core, core),
            (left_twin, 1 - core, 2 + core),
            (twin, 1 - core, 6),
        )
    ):
        send(fgs.at[cc], g_slot(x, core), g_send.at[i], g_recv.at[slot_at], where)
    fgb[pl.ds(pl.multiple_of(me * TOK, TOK), TOK)] = fgs[core]
    for i, from_x in enumerate((xr, xl, xo)):
        arrived(w_slot((xl, xr, xo)[i], core), w_recv.at[i])
        send(w_slot((xl, xr, xo)[i], core), w_slot((xl, xr, xo)[i], core), w_send.at[4 + i], w_recv.at[4 + i], twin)
    arrived(g_slot(xl, 0), g_recv.at[0])
    send(g_slot(xl, 0), g_slot(xl, 0), g_send.at[5], g_recv.at[4], right)
    arrived(g_slot(xr, 1), g_recv.at[3])
    send(g_slot(xr, 1), g_slot(xr, 1), g_send.at[6], g_recv.at[5], left)
    arrived(w_slot(x, 1 - core), w_recv.at[3])
    for i in range(3):
        arrived(w_slot((xl, xr, xo)[i], 1 - core), w_recv.at[4 + i])
    arrived(g_slot(xl, 1), g_recv.at[1])
    arrived(g_slot(xr, 0), g_recv.at[2])
    arrived(g_slot(x, 1 - core), g_recv.at[6])
    arrived(g_slot(xo, 0), g_recv.at[4])
    arrived(g_slot(xo, 1), g_recv.at[5])
    terms = jnp.dot(wbuf[...], fgb[...], preferred_element_type=F32) * (1.0 / (2 * NZ))
    for b in range(NY):
        for i in range(PAD // 16):
            for j in range(HALF // 128):
                low = b * PAD + 16 * i
                part[b, 3 * i + j] = terms[low : low + 16, 128 * j : 128 * (j + 1)].astype(BF16)
        part[b, 15] = jnp.zeros((16, 128), BF16)

    def added(ref):
        out = ref[0].astype(F32)
        for i in range(1, 8):
            out += ref[i].astype(F32)
        return out

    for i in range(1, 8):
        to_y, to_z = lax.rem(y + i, NY), lax.rem(z + i, NZ)
        send(part.at[to_y, pl.ds(0, 8)], yb1.at[y], t_send.at[0, i], t_recv.at[0, y], on_y[i - 1])
        send(part.at[:, 8 + to_z], zb1.at[z], t_send.at[1, i], t_recv.at[1, z], on_z[i - 1])
    yb1[y] = part[y, 0:8]
    zb1[z] = part[:, 8 + z]
    for i in range(1, 8):
        from_y = lax.rem(y + i, NY)
        arrived(yb1.at[from_y], t_recv.at[0, from_y])
    s1[...] = added(yb1).astype(BF16)
    for i in range(1, 8):
        to_z = lax.rem(z + i, NZ)
        send(s1.at[to_z], zb2.at[z], u_send.at[0, i], u_recv.at[0, z], on_z[i - 1])
    for i in range(1, 8):
        from_z = lax.rem(z + i, NZ)
        arrived(zb1.at[from_z], t_recv.at[1, from_z])
    s2[...] = added(zb1).astype(BF16)
    for i in range(1, 8):
        to_y = lax.rem(y + i, NY)
        send(s2.at[to_y], yb2.at[y], u_send.at[1, i], u_recv.at[1, y], on_y[i - 1])
    zb2[z] = s1[z]
    yb2[y] = s2[y]
    for i in range(1, 8):
        from_z = lax.rem(z + i, NZ)
        arrived(zb2.at[from_z], u_recv.at[0, from_z])
    fin[z, 0] = added(zb2).astype(BF16)
    for i in range(1, 8):
        from_y = lax.rem(y + i, NY)
        arrived(yb2.at[from_y], u_recv.at[1, from_y])
    fin[z, 1] = added(yb2).astype(BF16)
    for i in range(1, 8):
        send(fin.at[z], fin.at[z], f_send.at[i], f_recv.at[z], on_z[i - 1])
    for i in range(1, 8):
        from_z = lax.rem(z + i, NZ)
        arrived(fin.at[from_z], f_recv.at[from_z])
    send(fin, fin_sib, c_sem.at[0], c_sem.at[1], twin)
    arrived(fin_sib, c_sem.at[1])
    for half in range(2):
        mine = jnp.where(core == half, fin[...].astype(F32), fin_sib[...].astype(F32))
        wide = [
            jnp.concatenate([mine[(3 * i + j) % 8, (3 * i + j) // 8] for j in range(3)], axis=1)
            for i in range(PAD // 16)
        ]
        wide = jnp.concatenate(wide, axis=0)
        for k in range(3):
            cg_out[k, :, half * HALF : (half + 1) * HALF] = wide[k * SPAN : (k + 1) * SPAN]

    for one in sends:
        one.wait_send()


def on_device(input_rows, features, norm_gain, w_query, w_key, w_value, temper, head_grads):
    vmem = pl.BlockSpec(memory_space=pltpu.VMEM)
    dma = pltpu.SemaphoreType.DMA

    def scratch(*shape, dtype=BF16):
        return pltpu.VMEM(shape, dtype)

    fg, cg = pl.pallas_call(
        kernel,
        out_shape=(
            jax.ShapeDtypeStruct((TOK, CH), BF16),
            jax.ShapeDtypeStruct((3, SPAN, CH), F32),
        ),
        in_specs=[vmem] * 6 + [pl.BlockSpec(memory_space=pltpu.SMEM), vmem],
        out_specs=(vmem, vmem),
        scratch_shapes=[
            scratch(16, CH),
            scratch(4, HEADS, TOK, HS),
            scratch(8, QROWS, HS),
            scratch(8, QROWS, HS),
            scratch(2, QROWS, HS),
            scratch(2, TOK, HEADS * HS, dtype=F32),
            scratch(NX, NY * PAD, TOK),
            scratch(NY * PAD, 8 * TOK),
            scratch(8, QROWS, QROWS, dtype=F32),
            scratch(8, QROWS, QROWS, dtype=F32),
            scratch(8, QROWS, HS),
            scratch(8, QROWS, HS),
            scratch(NX, QROWS, HS),
            scratch(NX, QROWS, HS),
            scratch(3, QROWS, HS),
            scratch(3, QROWS, HS),
            scratch(3, QROWS, HS),
            scratch(3, QROWS, HS),
            scratch(3, QROWS, HS),
            scratch(3, HEADS, TOK, HS),
            scratch(3, TOK, HEADS * HS),
            scratch(2, TOK, HALF),
            scratch(8 * TOK, HALF),
            scratch(NY, 16, 16, 128),
            scratch(NY, 8, 16, 128),
            scratch(NZ, 8, 16, 128),
            scratch(8, 16, 128),
            scratch(8, 16, 128),
            scratch(NZ, 16, 128),
            scratch(NY, 16, 128),
            scratch(NZ, 2, 16, 128),
            scratch(NZ, 2, 16, 128),
            dma((2,)),
            dma((4, 4)), dma((4, 4)),
            dma((2, 19)), dma((2, 19)),
            dma((7,)), dma((7,)),
            dma((4,)), dma((4,)),
            dma((2, 4)), dma((2, 4)),
            dma((3,)), dma((3,)),
            dma((2, 3)), dma((2, 3)),
            dma((3, 4)), dma((3, 4)),
            dma((7,)), dma((7,)),
            dma((2, 8)), dma((2, 8)),
            dma((2, 8)), dma((2, 8)),
            dma((8,)), dma((8,)),
            dma((2,)),
        ],
        compiler_params=pltpu.CompilerParams(
            collective_id=0, has_side_effects=True, vmem_limit_bytes=56 * 1024 * 1024
        ),
    )(
        input_rows[0], features[0], norm_gain.reshape(1, CH), w_query, w_key, w_value, temper, head_grads[0],
    )
    return fg[None], cg


def solution(mesh):
    return jax.shard_map(
        on_device,
        mesh=mesh,
        in_specs=(
            P("dp", "seq", None),
            P("dp", "seq", None),
            P(),
            P(),
            P(),
            P(),
            P(),
            P("dp", "seq", None),
        ),
        out_specs=(P("dp", "seq", None), P(None, "seq", None)),
        check_vma=False,
    )
```

time: 120 us -> 95.9 us (0.80)
  Pallas kernels: 115 us -> 91.5 us
    pallas_call x1, Pallas kernels: 115 us -> 91.5 us  [on_device(): pl.pallas_call(kernel, out_shape=(jax.ShapeDtypeStruct((TOK, CH), BF16),...]
where the time goes in v2:
time: 95.9 us; the launch traced here: 95.7 us
  Pallas kernels  91.5 us (95%)
  local copies, waits for them, and re-layouts  3.61 us (4%)
    pallas_call x1, Pallas kernels, on_device(): pl.pallas_call(kernel, out_shape=(jax.ShapeDtypeStruct((TOK, CH), BF16),...  91.5 us
    unnamed x6, local copies, waits for them, and re-layouts  3.03 us

profile of v2, /device:TPU:1, one launch (start us, length us, event | category | flops | bytes accessed | tf_op | source)
XLA Modules:
  0.0 95.7 jit_solution(13171295301856996780)
XLA Ops:
  0.6 0.0 copy-start.1
  0.6 0.7 copy-done.1
  1.3 0.6 reshape.7.gain_ref
  1.9 91.5 %shard_map.95 = (bf16[128,768]{1,0:T(8,128)(2,1)}, f32[3,24,768]{2,1,0:T(8,128)}) custom-call(bf16[256,768]{1,0:T(8,128)(2,1)} %bitcast.4, bf16[128,768]{1,0:T(8,128)(2,1)} %bitcast.6, f32[1,768]{1,0:T(1,128)} %reshape.7.gain_ref, bf16[768,512]{1,0:T(8,128)(2,1)} %wq_ref.1, bf16[768,512]{1,0:T(8,128)(2,1)} %wk_ref.1, bf16[768,512]{1,0:T(8,128)(2,1)} %wv_ref.1, ...), custom_call_target="tpu_custom_call" | custom-call | tf_op jit(solution)/shard_map/pallas_call | solution.py:456
  93.4 0.0 copy-start
  93.4 1.7 %copy.12 = bf16[1,128,768]{2,1,0:T(8,128)(2,1)} copy(bf16[1,128,768]{2,1,0:T(8,128)(2,1)} %bitcast.5) | data formatting | bytes 393216
  95.0 0.0 copy-done
  95.0 0.7 copy.13
Async XLA Ops:
  0.6 0.7 copy-start.1
  93.4 1.7 %copy-start = (f32[3,24,768]{2,1,0:T(8,128)S(1)}, f32[3,24,768]{2,1,0:T(8,128)}, u32[]{:S(2)}) copy-start(f32[3,24,768]{2,1,0:T(8,128)} %get-tuple-element.9) | copy-start | bytes 663556

commit v3 on v2

--- a/solution.py
+++ b/solution.py
@@ -19,6 +19,12 @@
 SPAN = CH // (NX * NY)
 PAD = 80
 HALF = CH // 2
+QUARTER = CH // NX
+TILES = (
+    ((False, 0), (False, 1), (False, 2), (True, 0), (True, 4)),
+    ((False, 3), (False, 4), (False, 5), (True, 2), (True, 6)),
+    ((False, 6), (False, 7), (True, 1), (True, 3), (True, 5)),
+)
 
 
 def unit_rows(raw):
@@ -31,12 +37,12 @@
 
 
 def kernel(
-    rows_ref, feat_ref, gain_ref, wq_ref, wk_ref, wv_ref, temper_ref, hg_ref,
+    rows_hbm, feat_ref, gain_ref, wq_hbm, wk_ref, wv_hbm, temper_ref, hg_hbm,
     fg_out, cg_out,
-    prev, outgoing, keys, vals, qg, raw, wt, wbuf, e_buf, gp_buf, dv, dk, sib_v, sib_k, st_v, st_k, in_v, in_k,
-    total, back, dall, fgs, fgb, part, yb1, zb1, s1, s2, zb2, yb2, fin, fin_sib,
+    rows_ref, wq_ref, wv_ref, hg_ref, prev, outgoing, keys, vals, qg, raw, wt, wbuf, e_buf, gp_buf, dv, dk, sib_v, sib_k, st_v, st_k, in_v, in_k,
+    total, back, dall, fgs, fgb, tiles_y, tiles_z, yb1, zb1, s1, s2, zb2, yb2, fin, fin_sib,
     prev_sem, a_send, a_recv, k_send, k_recv, w_send, w_recv, sv_send, sv_recv, sk_send, sk_recv,
-    mv_send, mv_recv, mk_send, mk_recv, b_send, b_recv, g_send, g_recv, t_send, t_recv, u_send, u_recv, f_send, f_recv, c_sem,
+    mv_send, mv_recv, mk_send, mk_recv, b_send, b_recv, g_send, g_recv, t_send, t_recv, tz_send, tz_recv, u_send, u_recv, f_send, f_recv, c_sem, in_sem,
 ):
     seq, dp = lax.axis_index("seq"), lax.axis_index("dp")
     x, y = lax.div(seq, NY), lax.rem(seq, NY)
@@ -77,6 +83,10 @@
     on_y = [(at(x, lax.rem(y + i, NY)), dp) for i in range(1, NY)]
     on_z = [(seq, lax.rem(dp + 2 * i, 2 * NZ)) for i in range(1, NZ)]
 
+    staged = []
+    for i, (src, dst) in enumerate(((wv_hbm, wv_ref), (hg_hbm, hg_ref), (wq_hbm, wq_ref), (rows_hbm, rows_ref))):
+        staged.append(pltpu.make_async_copy(src, dst, in_sem.at[i]))
+        staged[i].start()
     barrier = pltpu.get_barrier_semaphore()
     partners = servers + owners + [ring_next, ring_prev, right, left, twin, far, right_twin, left_twin] + on_y + on_z
     for where in partners:
@@ -84,21 +94,14 @@
 
     feats = feat_ref[...].astype(F32)
     inv_rms = lax.rsqrt(jnp.mean(feats * feats, axis=1, keepdims=True) + EPSILON)
-    gain = gain_ref[...]
+    gain = gain_ref[...].reshape(1, CH)
     normed = (feats * inv_rms * gain).astype(BF16)
     slot = lax.div(y, 2)
     their_me = 2 * x + 1 - lax.rem(y, 2)
 
     def start_heads(kind, to):
-        started = []
         for i in range(HEADS):
-            started.append(copy(outgoing.at[kind, i], to, a_send.at[kind, i], a_recv.at[kind, slot], servers[i]))
-            started[i].start()
-        return started
-
-    def wait_heads(started):
-        for one in started:
-            one.wait_send()
+            send(outgoing.at[kind, i], to, a_send.at[kind, i], a_recv.at[kind, slot], servers[i])
 
     def project(which, w_ref):
         raw[which] = jnp.dot(normed, w_ref[...], preferred_element_type=F32)
@@ -108,32 +111,59 @@
     project(0, wk_ref)
     pl.semaphore_wait(barrier, len(partners))
     slot_rows = pl.ds(pl.multiple_of(slot * TOK, TOK), TOK)
-    sent = start_heads(0, keys.at[their_me, slot_rows])
+    start_heads(0, keys.at[their_me, slot_rows])
+    staged[3].wait()
     send(rows_ref.at[pl.ds(2 * TOK - 16, 16)], prev, prev_sem.at[0], prev_sem.at[1], ring_next)
-    project(1, wq_ref)
+    staged[0].wait()
+    staged[1].wait()
     values = jnp.dot(normed, wv_ref[...], preferred_element_type=F32).astype(BF16)
     for i in range(HEADS):
         outgoing[2, i] = values[:, i * HS : (i + 1) * HS]
         outgoing[3, i] = hg_ref[:, i * HS : (i + 1) * HS]
-    wait_heads(sent)
-    sent = start_heads(1, qg.at[0, slot_rows])
-
+    start_heads(2, vals.at[their_me, slot_rows])
+    staged[2].wait()
+    project(1, wq_ref)
+
+    def chosen(rows, columns, first_tap):
+        row = lax.broadcasted_iota(jnp.int32, (rows, columns), 0)
+        lane = lax.broadcasted_iota(jnp.int32, (rows, columns), 1)
+        return (row == 2 * lax.rem(lane, TOK) + lax.div(lane, TOK) + first_tap - 1).astype(F32).astype(BF16)
+
+    def w_slot(first_tap, taps, xx, cc):
+        return wbuf.at[pl.ds(first_tap, taps), :, pl.ds(pl.multiple_of((2 * xx + cc) * TOK, TOK), TOK)]
+
+    def put_windows(tap, windows):
+        for i in range(NX):
+            wt[i, tap] = windows[i * QUARTER : (i + 1) * QUARTER].astype(BF16)
+        wbuf[tap, :, pl.ds(pl.multiple_of(me * TOK, TOK), TOK)] = wt[x, tap]
+
+    def start_windows(group, first_tap, taps):
+        some = pl.ds(first_tap, taps)
+        for i, (to_x, where) in enumerate(((xl, left), (xr, right), (xo, far), (x, twin))):
+            src = wt.at[to_x, some]
+            send(src, w_slot(first_tap, taps, x, core), w_send.at[group, i], w_recv.at[group, i], where)
+
+    def windows_on(group, first_tap, taps):
+        for i, from_x in enumerate((xr, xl, xo)):
+            piece = w_slot(first_tap, taps, from_x, core)
+            arrived(piece, w_recv.at[group, i])
+            send(piece, piece, w_send.at[group, 4 + i], w_recv.at[group, 4 + i], twin)
+
+    def got_windows(group, first_tap, taps):
+        for i, from_x in enumerate((x, xr, xl, xo)):
+            arrived(w_slot(first_tap, taps, from_x, 1 - core), w_recv.at[group, 3 + i])
+
+    windows = lax.dot_general(rows_ref[...], chosen(2 * TOK, 2 * TOK, 1), FIRST_BOTH, preferred_element_type=F32)
+    put_windows(1, windows[:, 0:TOK])
+    put_windows(2, windows[:, TOK:])
+    start_windows(0, 1, 2)
+    start_heads(1, qg.at[0, slot_rows])
     arrived(prev, prev_sem.at[1])
-    row = lax.broadcasted_iota(jnp.int32, (2 * TOK, 3 * TOK), 0)
-    lane = lax.broadcasted_iota(jnp.int32, (2 * TOK, 3 * TOK), 1)
-    chosen = (row == 2 * lax.rem(lane, TOK) + lax.div(lane, TOK) - 1).astype(F32).astype(BF16)
-    taps = lax.dot_general(rows_ref[...], chosen, FIRST_BOTH, preferred_element_type=F32)
     row = lax.broadcasted_iota(jnp.int32, (16, TOK), 0)
     lane = lax.broadcasted_iota(jnp.int32, (16, TOK), 1)
     first = ((row == 15) & (lane == 0) & (seq > 0)).astype(F32).astype(BF16)
-    tap0 = taps[:, 0:TOK] + lax.dot_general(prev[...], first, FIRST_BOTH, preferred_element_type=F32)
-    three = (tap0, taps[:, TOK : 2 * TOK], taps[:, 2 * TOK :])
-    zeros = jnp.zeros((PAD - 3 * SPAN, TOK), F32)
-    for i in range(NX):
-        for j in range(NY):
-            low = (i * NY + j) * SPAN
-            block = jnp.concatenate([tap[low : low + SPAN] for tap in three] + [zeros], axis=0)
-            wt[i, j * PAD : (j + 1) * PAD] = block.astype(BF16)
+    windows = lax.dot_general(rows_ref[...], chosen(2 * TOK, TOK, 0), FIRST_BOTH, preferred_element_type=F32)
+    put_windows(0, windows + lax.dot_general(prev[...], first, FIRST_BOTH, preferred_element_type=F32))
 
     def chunk(ref, block, i):
         j = lax.rem(slot + (0, 1, 3, 2)[i], 4)
@@ -173,14 +203,11 @@
     def got_from_twin(t, k):
         arrived(both[t].at[(twin_left, twin_right, twin_far)[k]], k_recv.at[t, 16 + k])
 
-    ring_own(0, 0)
-    ring_own(0, 1)
-    wait_heads(sent)
-    sent = start_heads(2, vals.at[their_me, slot_rows])
-    ring_own(0, 2)
-    ring_own(0, 3)
-    wait_heads(sent)
-    sends += start_heads(3, qg.at[1, slot_rows])
+    for i in range(4):
+        ring_own(0, i)
+    start_heads(3, qg.at[1, slot_rows])
+    for i in range(4):
+        ring_own(1, i)
     ring_on(0)
 
     for j in range(4):
@@ -194,20 +221,16 @@
         return exp_sum + jnp.sum(expo, axis=0, keepdims=True)
 
     exp_sum = score_pass(me, jnp.zeros((1, QROWS), F32))
-    ring_own(1, 0)
     got_twin(0)
     exp_sum = score_pass(twin_me, exp_sum)
-    ring_own(1, 1)
+    ring_on(1)
     exp_sum = score_pass(from_left, exp_sum)
-    ring_own(1, 2)
     exp_sum = score_pass(from_right, exp_sum)
-    ring_own(1, 3)
     ring_far(0)
     got_from_twin(0, 0)
     exp_sum = score_pass(twin_left, exp_sum)
     got_from_twin(0, 1)
     exp_sum = score_pass(twin_right, exp_sum)
-    ring_on(1)
     exp_sum = score_pass(from_far, exp_sum)
     got_from_twin(0, 2)
     exp_sum = score_pass(twin_far, exp_sum)
@@ -257,6 +280,8 @@
             got_from_twin(1, 2)
             dot_sum = prob_grad(twin_far, dot_sum)
 
+    windows_on(0, 1, 2)
+
     grad_dot = dot_sum * inv_sum
     inv_factor = inv_sum * factor
     half_rows = QROWS // 2
@@ -281,6 +306,20 @@
             st_k[i, low:high] = summed.astype(BF16)
             send(half_of(st_k, i, half), half_of(in_k, i, half), mk_send.at[half, i], mk_recv.at[half, i], to[i])
         return summed
+
+    def start_back(kind, j):
+        src = total.at[kind, pl.ds(j * TOK, TOK)]
+        send(src, back.at[kind, head], b_send.at[kind, j], b_recv.at[kind, head], owners[j])
+
+    def finish_values():
+        arrived(sib_v.at[3], sv_recv.at[3])
+        summed = dv[me].astype(F32) + sib_v[3].astype(F32)
+        for i in range(3):
+            arrived(in_v.at[i], mv_recv.at[i])
+            summed += in_v[i].astype(F32)
+        total[2] = summed.astype(BF16)
+        for j in range(4):
+            start_back(2, j)
 
     grad_query = jnp.zeros((HS, QROWS), F32)
     pending = None
@@ -293,22 +332,12 @@
             if pending is not None and pending[1] < 3:
                 pass_keys(*pending)
             pending = (half, i)
+            if pending == (1, 2):
+                finish_values()
     total[0] = jnp.transpose(grad_query).astype(BF16)
-
-    def start_back(kind, j):
-        src = total.at[kind, pl.ds(j * TOK, TOK)]
-        send(src, back.at[kind, head], b_send.at[kind, j], b_recv.at[kind, head], owners[j])
 
     for j in range(4):
         start_back(0, j)
-    arrived(sib_v.at[3], sv_recv.at[3])
-    summed = dv[me].astype(F32) + sib_v[3].astype(F32)
-    for i in range(3):
-        arrived(in_v.at[i], mv_recv.at[i])
-        summed += in_v[i].astype(F32)
-    total[2] = summed.astype(BF16)
-    for j in range(4):
-        start_back(2, j)
     for half in range(2):
         low = half * half_rows
         high = low + half_rows
@@ -320,13 +349,7 @@
         for j in range(2 * half, 2 * half + 2):
             start_back(1, j)
 
-    def w_slot(xx, cc):
-        return wbuf.at[:, pl.ds(pl.multiple_of((2 * xx + cc) * TOK, TOK), TOK)]
-
-    for i, where in enumerate((right, left, far)):
-        send(wt.at[(xr, xl, xo)[i]], w_slot(x, core), w_send.at[i], w_recv.at[i], where)
-    send(wt.at[x], w_slot(x, core), w_send.at[3], w_recv.at[3], twin)
-    wbuf[:, pl.ds(pl.multiple_of(me * TOK, TOK), TOK)] = wt[x]
+    start_windows(1, 0, 1)
 
     def put_raw_grad(which, i, upstream_grad):
         unit, inv = unit_rows(raw[1 - which, :, i * HS : (i + 1) * HS])
@@ -349,45 +372,68 @@
     feature_grad = inv_rms * (gained - unit_feats * jnp.mean(unit_feats * gained, axis=1, keepdims=True))
     feature_grad = feature_grad.astype(BF16)
     fg_out[...] = feature_grad
-    fgs[0] = feature_grad[:, 0:HALF]
-    fgs[1] = feature_grad[:, HALF:]
-
-    def g_slot(xx, cc):
-        return rows_of(fgb, (2 * xx + cc) * TOK, TOK)
-
-    for i, (where, cc, slot_at) in enumerate(
-        (
-            (right, core, core),
-            (left, core, 2 + core),
-            (right_twin, 1 - core, core),
-            (left_twin, 1 - core, 2 + core),
-            (twin, 1 - core, 6),
-        )
-    ):
-        send(fgs.at[cc], g_slot(x, core), g_send.at[i], g_recv.at[slot_at], where)
-    fgb[pl.ds(pl.multiple_of(me * TOK, TOK), TOK)] = fgs[core]
-    for i, from_x in enumerate((xr, xl, xo)):
-        arrived(w_slot((xl, xr, xo)[i], core), w_recv.at[i])
-        send(w_slot((xl, xr, xo)[i], core), w_slot((xl, xr, xo)[i], core), w_send.at[4 + i], w_recv.at[4 + i], twin)
-    arrived(g_slot(xl, 0), g_recv.at[0])
-    send(g_slot(xl, 0), g_slot(xl, 0), g_send.at[5], g_recv.at[4], right)
-    arrived(g_slot(xr, 1), g_recv.at[3])
-    send(g_slot(xr, 1), g_slot(xr, 1), g_send.at[6], g_recv.at[5], left)
-    arrived(w_slot(x, 1 - core), w_recv.at[3])
-    for i in range(3):
-        arrived(w_slot((xl, xr, xo)[i], 1 - core), w_recv.at[4 + i])
-    arrived(g_slot(xl, 1), g_recv.at[1])
-    arrived(g_slot(xr, 0), g_recv.at[2])
-    arrived(g_slot(x, 1 - core), g_recv.at[6])
-    arrived(g_slot(xo, 0), g_recv.at[4])
-    arrived(g_slot(xo, 1), g_recv.at[5])
-    terms = jnp.dot(wbuf[...], fgb[...], preferred_element_type=F32) * (1.0 / (2 * NZ))
-    for b in range(NY):
-        for i in range(PAD // 16):
-            for j in range(HALF // 128):
-                low = b * PAD + 16 * i
-                part[b, 3 * i + j] = terms[low : low + 16, 128 * j : 128 * (j + 1)].astype(BF16)
-        part[b, 15] = jnp.zeros((16, 128), BF16)
+    for i in range(2):
+        for k in range(3):
+            fgs[i, k] = feature_grad[:, i * HALF + k * 128 : i * HALF + (k + 1) * 128]
+
+    def g_slot(k, xx, cc):
+        return fgb.at[k, pl.ds(pl.multiple_of((2 * xx + cc) * TOK, TOK), TOK)]
+
+    for k in range(3):
+        for i, (where, cc, slot_at) in enumerate(
+            (
+                (right, core, core),
+                (left, core, 2 + core),
+                (right_twin, 1 - core, core),
+                (left_twin, 1 - core, 2 + core),
+                (twin, 1 - core, 6),
+            )
+        ):
+            send(fgs.at[cc, k], g_slot(k, x, core), g_send.at[k, i], g_recv.at[k, slot_at], where)
+        fgb[k, pl.ds(pl.multiple_of(me * TOK, TOK), TOK)] = fgs[core, k]
+    windows_on(1, 0, 1)
+
+    def gather_on(k):
+        arrived(g_slot(k, xl, 0), g_recv.at[k, 0])
+        send(g_slot(k, xl, 0), g_slot(k, xl, 0), g_send.at[k, 5], g_recv.at[k, 4], right)
+        arrived(g_slot(k, xr, 1), g_recv.at[k, 3])
+        send(g_slot(k, xr, 1), g_slot(k, xr, 1), g_send.at[k, 6], g_recv.at[k, 5], left)
+
+    def sum_chunk(k):
+        arrived(g_slot(k, xl, 1), g_recv.at[k, 1])
+        arrived(g_slot(k, xr, 0), g_recv.at[k, 2])
+        arrived(g_slot(k, x, 1 - core), g_recv.at[k, 6])
+        arrived(g_slot(k, xo, 0), g_recv.at[k, 4])
+        arrived(g_slot(k, xo, 1), g_recv.at[k, 5])
+        terms = jnp.dot(wbuf[...].reshape(3 * QUARTER, 8 * TOK), fgb[k], preferred_element_type=F32) * (1.0 / (2 * NZ))
+        for b in range(NY):
+            taps = [terms[i * QUARTER + b * SPAN : i * QUARTER + (b + 1) * SPAN] for i in range(3)]
+            rows = jnp.concatenate(taps + [jnp.zeros((PAD - 3 * SPAN, 128), F32)], axis=0).astype(BF16)
+            for i, (by_z, at_tile) in enumerate(TILES[k]):
+                tile = rows[16 * i : 16 * (i + 1)]
+                if by_z:
+                    tiles_z[at_tile, b] = tile
+                else:
+                    tiles_y[b, at_tile] = tile
+        of_y = [at_tile for by_z, at_tile in TILES[k] if not by_z]
+        some = pl.ds(of_y[0], len(of_y))
+        for i in range(1, NY):
+            to_y = lax.rem(y + i, NY)
+            send(tiles_y.at[to_y, some], yb1.at[y, some], t_send.at[k, i], t_recv.at[k, y], on_y[i - 1])
+        yb1[y, some] = tiles_y[y, some]
+        for by_z, at_tile in TILES[k]:
+            if by_z:
+
+                @pl.when(z != at_tile)
+                def _():
+                    to_owner(at_tile).start()
+
+                @pl.when(z == at_tile)
+                def _():
+                    zb1[z] = tiles_z[at_tile]
+
+    def to_owner(at_tile):
+        return copy(tiles_z.at[at_tile], zb1.at[z], tz_send.at[at_tile], tz_recv.at[z], (seq, 2 * at_tile + core))
 
     def added(ref):
         out = ref[0].astype(F32)
@@ -395,22 +441,34 @@
             out += ref[i].astype(F32)
         return out
 
-    for i in range(1, 8):
-        to_y, to_z = lax.rem(y + i, NY), lax.rem(z + i, NZ)
-        send(part.at[to_y, pl.ds(0, 8)], yb1.at[y], t_send.at[0, i], t_recv.at[0, y], on_y[i - 1])
-        send(part.at[:, 8 + to_z], zb1.at[z], t_send.at[1, i], t_recv.at[1, z], on_z[i - 1])
-    yb1[y] = part[y, 0:8]
-    zb1[z] = part[:, 8 + z]
-    for i in range(1, 8):
+    @pl.when(z == NZ - 1)
+    def _():
+        zb1[...] = jnp.zeros_like(zb1)
+
+    gather_on(0)
+    gather_on(1)
+    got_windows(0, 1, 2)
+    got_windows(1, 0, 1)
+    sum_chunk(0)
+    gather_on(2)
+    sum_chunk(1)
+    sum_chunk(2)
+    for i in range(1, NY):
         from_y = lax.rem(y + i, NY)
-        arrived(yb1.at[from_y], t_recv.at[0, from_y])
+        for k in range(3):
+            of_y = [at_tile for by_z, at_tile in TILES[k] if not by_z]
+            arrived(yb1.at[from_y, pl.ds(of_y[0], len(of_y))], t_recv.at[k, from_y])
     s1[...] = added(yb1).astype(BF16)
     for i in range(1, 8):
         to_z = lax.rem(z + i, NZ)
         send(s1.at[to_z], zb2.at[z], u_send.at[0, i], u_recv.at[0, z], on_z[i - 1])
-    for i in range(1, 8):
-        from_z = lax.rem(z + i, NZ)
-        arrived(zb1.at[from_z], t_recv.at[1, from_z])
+
+    @pl.when(z < NZ - 1)
+    def _():
+        for i in range(1, 8):
+            from_z = lax.rem(z + i, NZ)
+            arrived(zb1.at[from_z], tz_recv.at[from_z])
+
     s2[...] = added(zb1).astype(BF16)
     for i in range(1, 8):
         to_y = lax.rem(y + i, NY)
@@ -434,20 +492,25 @@
     arrived(fin_sib, c_sem.at[1])
     for half in range(2):
         mine = jnp.where(core == half, fin[...].astype(F32), fin_sib[...].astype(F32))
-        wide = [
-            jnp.concatenate([mine[(3 * i + j) % 8, (3 * i + j) // 8] for j in range(3)], axis=1)
-            for i in range(PAD // 16)
-        ]
+        wide = []
+        for i in range(PAD // 16):
+            row = [TILES[k][i] for k in range(3)]
+            wide.append(jnp.concatenate([mine[at_tile, int(by_z)] for by_z, at_tile in row], axis=1))
         wide = jnp.concatenate(wide, axis=0)
         for k in range(3):
             cg_out[k, :, half * HALF : (half + 1) * HALF] = wide[k * SPAN : (k + 1) * SPAN]
 
     for one in sends:
         one.wait_send()
+    for at_tile in range(NZ - 1):
+
+        @pl.when(z != at_tile)
+        def _():
+            to_owner(at_tile).wait_send()
 
 
 def on_device(input_rows, features, norm_gain, w_query, w_key, w_value, temper, head_grads):
-    vmem = pl.BlockSpec(memory_space=pltpu.VMEM)
+    vmem, hbm = pl.BlockSpec(memory_space=pltpu.VMEM), pl.BlockSpec(memory_space=pl.ANY)
     dma = pltpu.SemaphoreType.DMA
 
     def scratch(*shape, dtype=BF16):
@@ -459,17 +522,21 @@
             jax.ShapeDtypeStruct((TOK, CH), BF16),
             jax.ShapeDtypeStruct((3, SPAN, CH), F32),
         ),
-        in_specs=[vmem] * 6 + [pl.BlockSpec(memory_space=pltpu.SMEM), vmem],
+        in_specs=[hbm, vmem, vmem, hbm, vmem, hbm, pl.BlockSpec(memory_space=pltpu.SMEM), hbm],
         out_specs=(vmem, vmem),
         scratch_shapes=[
+            scratch(2 * TOK, CH),
+            scratch(CH, HEADS * HS),
+            scratch(CH, HEADS * HS),
+            scratch(TOK, HEADS * HS),
             scratch(16, CH),
             scratch(4, HEADS, TOK, HS),
             scratch(8, QROWS, HS),
             scratch(8, QROWS, HS),
             scratch(2, QROWS, HS),
             scratch(2, TOK, HEADS * HS, dtype=F32),
-            scratch(NX, NY * PAD, TOK),
-            scratch(NY * PAD, 8 * TOK),
+            scratch(NX, 3, QUARTER, TOK),
+            scratch(3, QUARTER, 8 * TOK),
             scratch(8, QROWS, QROWS, dtype=F32),
             scratch(8, QROWS, QROWS, dtype=F32),
             scratch(8, QROWS, HS),
@@ -483,9 +550,10 @@
             scratch(3, QROWS, HS),
             scratch(3, HEADS, TOK, HS),
             scratch(3, TOK, HEADS * HS),
-            scratch(2, TOK, HALF),
-            scratch(8 * TOK, HALF),
-            scratch(NY, 16, 16, 128),
+            scratch(2, 3, TOK, 128),
+            scratch(3, 8 * TOK, 128),
+            scratch(NY, 8, 16, 128),
+            scratch(NZ, NY, 16, 128),
             scratch(NY, 8, 16, 128),
             scratch(NZ, 8, 16, 128),
             scratch(8, 16, 128),
@@ -497,23 +565,25 @@
             dma((2,)),
             dma((4, 4)), dma((4, 4)),
             dma((2, 19)), dma((2, 19)),
-            dma((7,)), dma((7,)),
+            dma((2, 7)), dma((2, 7)),
             dma((4,)), dma((4,)),
             dma((2, 4)), dma((2, 4)),
             dma((3,)), dma((3,)),
             dma((2, 3)), dma((2, 3)),
             dma((3, 4)), dma((3, 4)),
-            dma((7,)), dma((7,)),
-            dma((2, 8)), dma((2, 8)),
+            dma((3, 7)), dma((3, 7)),
+            dma((3, 8)), dma((3, 8)),
+            dma((8,)), dma((8,)),
             dma((2, 8)), dma((2, 8)),
             dma((8,)), dma((8,)),
             dma((2,)),
+            dma((4,)),
         ],
         compiler_params=pltpu.CompilerParams(
             collective_id=0, has_side_effects=True, vmem_limit_bytes=56 * 1024 * 1024
         ),
     )(
-        input_rows[0], features[0], norm_gain.reshape(1, CH), w_query, w_key, w_value, temper, head_grads[0],
+        input_rows[0], features[0], norm_gain, w_query, w_key, w_value, temper, head_grads[0],
     )
     return fg[None], cg
 

time: 95.9 us -> 92.9 us (0.969)
  Pallas kernels: 91.5 us -> 89.7 us
  local copies, waits for them, and re-layouts: 3.61 us -> 2.35 us
    pallas_call x1, Pallas kernels: 91.5 us -> 89.7 us  [on_device(): pl.pallas_call(kernel, out_shape=(jax.ShapeDtypeStruct((TOK, CH), BF16),...]
    unnamed x6 -> x4, local copies, waits for them, and re-layouts: 3.03 us -> 2.35 us
where the time goes in v3:
time: 92.9 us; the launch traced here: 92.7 us
  Pallas kernels  89.7 us (97%)
  local copies, waits for them, and re-layouts  2.35 us (3%)
    pallas_call x1, Pallas kernels, on_device(): pl.pallas_call(kernel, out_shape=(jax.ShapeDtypeStruct((TOK, CH), BF16),...  89.7 us
    unnamed x4, local copies, waits for them, and re-layouts  2.35 us

profile of v3, /device:TPU:1, one launch (start us, length us, event | category | flops | bytes accessed | tf_op | source)
XLA Modules:
  0.0 92.7 jit_solution(2397021034698295048)
XLA Ops:
  0.6 89.7 %shard_map.95 = (bf16[128,768]{1,0:T(8,128)(2,1)}, f32[3,24,768]{2,1,0:T(8,128)}) custom-call(bf16[256,768]{1,0:T(8,128)(2,1)} %bitcast.4, bf16[128,768]{1,0:T(8,128)(2,1)} %bitcast.5, f32[768]{0:T(1024)} %gain_ref.1, bf16[768,512]{1,0:T(8,128)(2,1)} %wq_hbm.1, bf16[768,512]{1,0:T(8,128)(2,1)} %wk_ref.1, bf16[768,512]{1,0:T(8,128)(2,1)} %wv_hbm.1, ...), custom_call_target="tpu_custom_call" | custom-call | tf_op jit(solution)/shard_map/pallas_call | solution.py:519
  90.4 0.0 copy-start
  90.4 1.7 %copy.12 = bf16[1,128,768]{2,1,0:T(8,128)(2,1)} copy(bf16[1,128,768]{2,1,0:T(8,128)(2,1)} %bitcast.6) | data formatting | bytes 393216
  92.0 0.0 copy-done
  92.0 0.7 copy.13
Async XLA Ops:
  90.4 1.7 %copy-start = (f32[3,24,768]{2,1,0:T(8,128)S(1)}, f32[3,24,768]{2,1,0:T(8,128)}, u32[]{:S(2)}) copy-start(f32[3,24,768]{2,1,0:T(8,128)} %get-tuple-element.9) | copy-start | bytes 663556

commit v4 on v3

--- a/solution.py
+++ b/solution.py
@@ -21,9 +21,9 @@
 HALF = CH // 2
 QUARTER = CH // NX
 TILES = (
-    ((False, 0), (False, 1), (False, 2), (True, 0), (True, 4)),
-    ((False, 3), (False, 4), (False, 5), (True, 2), (True, 6)),
-    ((False, 6), (False, 7), (True, 1), (True, 3), (True, 5)),
+    ((False, 0), (False, 1), (True, 0), (True, 3), (True, 6)),
+    ((False, 2), (False, 3), (False, 4), (True, 1), (True, 4)),
+    ((False, 5), (False, 6), (False, 7), (True, 2), (True, 5)),
 )
 
 
@@ -37,9 +37,9 @@
 
 
 def kernel(
-    rows_hbm, feat_ref, gain_ref, wq_hbm, wk_ref, wv_hbm, temper_ref, hg_hbm,
+    rows_hbm, feat_hbm, gain_hbm, wq_hbm, wk_hbm, wv_hbm, temper_hbm, hg_hbm,
     fg_out, cg_out,
-    rows_ref, wq_ref, wv_ref, hg_ref, prev, outgoing, keys, vals, qg, raw, wt, wbuf, e_buf, gp_buf, dv, dk, sib_v, sib_k, st_v, st_k, in_v, in_k,
+    rows_ref, feat_ref, gain_ref, wq_ref, wk_ref, wv_ref, temper_ref, hg_ref, prev, outgoing, keys, vals, qg, raw, wt, wbuf, e_buf, gp_buf, dv, dk, sib_v, sib_k, st_v, st_k, in_v, in_k,
     total, back, dall, fgs, fgb, tiles_y, tiles_z, yb1, zb1, s1, s2, zb2, yb2, fin, fin_sib,
     prev_sem, a_send, a_recv, k_send, k_recv, w_send, w_recv, sv_send, sv_recv, sk_send, sk_recv,
     mv_send, mv_recv, mk_send, mk_recv, b_send, b_recv, g_send, g_recv, t_send, t_recv, tz_send, tz_recv, u_send, u_recv, f_send, f_recv, c_sem, in_sem,
@@ -79,19 +79,27 @@
     owners = [(at(x, 2 * j + 1 - core), 2 * z + part_y) for j in range(4)]
     ring_next, ring_prev = (lax.rem(seq + 1, n_seq), dp), (lax.rem(seq + n_seq - 1, n_seq), dp)
     right, left, twin, far = (at(xr, y), dp), (at(xl, y), dp), (seq, sib), (at(xo, y), dp)
-    right_twin, left_twin = (at(xr, y), sib), (at(xl, y), sib)
+    right_twin, left_twin, far_twin = (at(xr, y), sib), (at(xl, y), sib), (at(xo, y), sib)
     on_y = [(at(x, lax.rem(y + i, NY)), dp) for i in range(1, NY)]
     on_z = [(seq, lax.rem(dp + 2 * i, 2 * NZ)) for i in range(1, NZ)]
 
+    barrier = pltpu.get_barrier_semaphore()
+    partners = servers + owners + [ring_next, ring_prev, right, left, twin, far, right_twin, left_twin, far_twin] + on_y + on_z
+    for where in partners:
+        pl.semaphore_signal(barrier, inc=1, device_id=where, device_id_type=MESH)
+
     staged = []
-    for i, (src, dst) in enumerate(((wv_hbm, wv_ref), (hg_hbm, hg_ref), (wq_hbm, wq_ref), (rows_hbm, rows_ref))):
+    for i, (src, dst) in enumerate(
+        (
+            (feat_hbm, feat_ref), (gain_hbm, gain_ref), (wk_hbm, wk_ref), (temper_hbm, temper_ref),
+            (wv_hbm, wv_ref), (hg_hbm, hg_ref), (rows_hbm, rows_ref), (wq_hbm, wq_ref),
+        )
+    ):
         staged.append(pltpu.make_async_copy(src, dst, in_sem.at[i]))
         staged[i].start()
-    barrier = pltpu.get_barrier_semaphore()
-    partners = servers + owners + [ring_next, ring_prev, right, left, twin, far, right_twin, left_twin] + on_y + on_z
-    for where in partners:
-        pl.semaphore_signal(barrier, inc=1, device_id=where, device_id_type=MESH)
-
+
+    for one in staged[:4]:
+        one.wait()
     feats = feat_ref[...].astype(F32)
     inv_rms = lax.rsqrt(jnp.mean(feats * feats, axis=1, keepdims=True) + EPSILON)
     gain = gain_ref[...].reshape(1, CH)
@@ -100,8 +108,15 @@
     their_me = 2 * x + 1 - lax.rem(y, 2)
 
     def start_heads(kind, to):
+        started = []
         for i in range(HEADS):
-            send(outgoing.at[kind, i], to, a_send.at[kind, i], a_recv.at[kind, slot], servers[i])
+            started.append(copy(outgoing.at[kind, i], to, a_send.at[kind, i], a_recv.at[kind, slot], servers[i]))
+            started[i].start()
+        return started
+
+    def wait_heads(started):
+        for one in started:
+            one.wait_send()
 
     def project(which, w_ref):
         raw[which] = jnp.dot(normed, w_ref[...], preferred_element_type=F32)
@@ -111,18 +126,15 @@
     project(0, wk_ref)
     pl.semaphore_wait(barrier, len(partners))
     slot_rows = pl.ds(pl.multiple_of(slot * TOK, TOK), TOK)
-    start_heads(0, keys.at[their_me, slot_rows])
-    staged[3].wait()
+    sent = start_heads(0, keys.at[their_me, slot_rows])
+    staged[6].wait()
     send(rows_ref.at[pl.ds(2 * TOK - 16, 16)], prev, prev_sem.at[0], prev_sem.at[1], ring_next)
-    staged[0].wait()
-    staged[1].wait()
+    staged[4].wait()
+    staged[5].wait()
     values = jnp.dot(normed, wv_ref[...], preferred_element_type=F32).astype(BF16)
     for i in range(HEADS):
         outgoing[2, i] = values[:, i * HS : (i + 1) * HS]
         outgoing[3, i] = hg_ref[:, i * HS : (i + 1) * HS]
-    start_heads(2, vals.at[their_me, slot_rows])
-    staged[2].wait()
-    project(1, wq_ref)
 
     def chosen(rows, columns, first_tap):
         row = lax.broadcasted_iota(jnp.int32, (rows, columns), 0)
@@ -157,7 +169,10 @@
     put_windows(1, windows[:, 0:TOK])
     put_windows(2, windows[:, TOK:])
     start_windows(0, 1, 2)
-    start_heads(1, qg.at[0, slot_rows])
+    wait_heads(sent)
+    sends += start_heads(2, vals.at[their_me, slot_rows])
+    staged[7].wait()
+    project(1, wq_ref)
     arrived(prev, prev_sem.at[1])
     row = lax.broadcasted_iota(jnp.int32, (16, TOK), 0)
     lane = lax.broadcasted_iota(jnp.int32, (16, TOK), 1)
@@ -203,11 +218,16 @@
     def got_from_twin(t, k):
         arrived(both[t].at[(twin_left, twin_right, twin_far)[k]], k_recv.at[t, 16 + k])
 
-    for i in range(4):
-        ring_own(0, i)
-    start_heads(3, qg.at[1, slot_rows])
-    for i in range(4):
-        ring_own(1, i)
+    ring_own(0, 0)
+    ring_own(0, 1)
+    sends += start_heads(1, qg.at[0, slot_rows])
+    ring_own(0, 2)
+    ring_own(0, 3)
+    ring_own(1, 0)
+    ring_own(1, 1)
+    sends += start_heads(3, qg.at[1, slot_rows])
+    ring_own(1, 2)
+    ring_own(1, 3)
     ring_on(0)
 
     for j in range(4):
@@ -261,25 +281,21 @@
         value_grad(block)
         send(dv.at[block], sib_v.at[i], sv_send.at[i], sv_recv.at[i], twin)
         value_grad(2 * order[i] + core)
-        if i > 0:
-            pass_values(i - 1)
-        if i == 0:
-            dot_sum = prob_grad(me, dot_sum)
-            got_twin(1)
-            dot_sum = prob_grad(twin_me, dot_sum)
-        elif i == 1:
-            dot_sum = prob_grad(from_left, dot_sum)
-            dot_sum = prob_grad(from_right, dot_sum)
-            ring_far(1)
-        elif i == 2:
-            for k, other in enumerate((twin_left, twin_right)):
-                got_from_twin(1, k)
-                dot_sum = prob_grad(other, dot_sum)
-        else:
-            dot_sum = prob_grad(from_far, dot_sum)
-            got_from_twin(1, 2)
-            dot_sum = prob_grad(twin_far, dot_sum)
-
+        if i > 1:
+            pass_values(i - 2)
+    dot_sum = prob_grad(me, dot_sum)
+    pass_values(2)
+    got_twin(1)
+    dot_sum = prob_grad(twin_me, dot_sum)
+    dot_sum = prob_grad(from_left, dot_sum)
+    dot_sum = prob_grad(from_right, dot_sum)
+    ring_far(1)
+    for k, other in enumerate((twin_left, twin_right)):
+        got_from_twin(1, k)
+        dot_sum = prob_grad(other, dot_sum)
+    dot_sum = prob_grad(from_far, dot_sum)
+    got_from_twin(1, 2)
+    dot_sum = prob_grad(twin_far, dot_sum)
     windows_on(0, 1, 2)
 
     grad_dot = dot_sum * inv_sum
@@ -390,6 +406,9 @@
             )
         ):
             send(fgs.at[cc, k], g_slot(k, x, core), g_send.at[k, i], g_recv.at[k, slot_at], where)
+        if k == 2:
+            for i, (where, cc) in enumerate(((far, core), (far_twin, 1 - core))):
+                send(fgs.at[cc, k], g_slot(k, x, core), g_send.at[k, 5 + i], g_recv.at[k, 4 + core], where)
         fgb[k, pl.ds(pl.multiple_of(me * TOK, TOK), TOK)] = fgs[core, k]
     windows_on(1, 0, 1)
 
@@ -450,7 +469,8 @@
     got_windows(0, 1, 2)
     got_windows(1, 0, 1)
     sum_chunk(0)
-    gather_on(2)
+    arrived(g_slot(2, xl, 0), g_recv.at[2, 0])
+    arrived(g_slot(2, xr, 1), g_recv.at[2, 3])
     sum_chunk(1)
     sum_chunk(2)
     for i in range(1, NY):
@@ -509,6 +529,11 @@
             to_owner(at_tile).wait_send()
 
 
+def publish(fg_in, cg_in, fg_out, cg_out):
+    fg_out[0] = fg_in[...]
+    cg_out[...] = cg_in[...]
+
+
 def on_device(input_rows, features, norm_gain, w_query, w_key, w_value, temper, head_grads):
     vmem, hbm = pl.BlockSpec(memory_space=pltpu.VMEM), pl.BlockSpec(memory_space=pl.ANY)
     dma = pltpu.SemaphoreType.DMA
@@ -522,12 +547,16 @@
             jax.ShapeDtypeStruct((TOK, CH), BF16),
             jax.ShapeDtypeStruct((3, SPAN, CH), F32),
         ),
-        in_specs=[hbm, vmem, vmem, hbm, vmem, hbm, pl.BlockSpec(memory_space=pltpu.SMEM), hbm],
+        in_specs=[hbm] * 8,
         out_specs=(vmem, vmem),
         scratch_shapes=[
             scratch(2 * TOK, CH),
+            scratch(TOK, CH),
+            scratch(CH, dtype=F32),
             scratch(CH, HEADS * HS),
             scratch(CH, HEADS * HS),
+            scratch(CH, HEADS * HS),
+            pltpu.SMEM((HEADS,), F32),
             scratch(TOK, HEADS * HS),
             scratch(16, CH),
             scratch(4, HEADS, TOK, HS),
@@ -577,7 +606,7 @@
             dma((2, 8)), dma((2, 8)),
             dma((8,)), dma((8,)),
             dma((2,)),
-            dma((4,)),
+            dma((8,)),
         ],
         compiler_params=pltpu.CompilerParams(
             collective_id=0, has_side_effects=True, vmem_limit_bytes=56 * 1024 * 1024
@@ -585,7 +614,15 @@
     )(
         input_rows[0], features[0], norm_gain, w_query, w_key, w_value, temper, head_grads[0],
     )
-    return fg[None], cg
+    return pl.pallas_call(
+        publish,
+        out_shape=(
+            jax.ShapeDtypeStruct((1, TOK, CH), BF16),
+            jax.ShapeDtypeStruct((3, SPAN, CH), F32),
+        ),
+        in_specs=[vmem, vmem],
+        out_specs=(vmem, vmem),
+    )(fg, cg)
 
 
 def solution(mesh):

time: 92.9 us -> 90.7 us (0.976)
  local copies, waits for them, and re-layouts: 2.35 us -> 0 us
    unnamed x4 -> x0, local copies, waits for them, and re-layouts: 2.35 us -> none
    pallas_call x0 -> x1, Pallas kernels: none -> 1.79 us  [on_device(): pl.pallas_call(publish, out_shape=(jax.ShapeDtypeStruct((1, TOK, CH), BF1...]
    pallas_call x1, Pallas kernels: 89.7 us -> 88.1 us  [on_device(): pl.pallas_call(kernel, out_shape=(jax.ShapeDtypeStruct((TOK, CH), BF16),...]
where the time goes in v4:
time: 90.7 us; the launch traced here: 90.5 us
  Pallas kernels  89.9 us (99%)
    pallas_call x1, Pallas kernels, on_device(): pl.pallas_call(kernel, out_shape=(jax.ShapeDtypeStruct((TOK, CH), BF16),...  88.1 us

profile of v4, /device:TPU:1, one launch (start us, length us, event | category | flops | bytes accessed | tf_op | source)
XLA Modules:
  0.0 90.5 jit_solution(12413930289374821833)
XLA Ops:
  0.6 88.1 %shard_map.95 = (bf16[128,768]{1,0:T(8,128)(2,1)}, f32[3,24,768]{2,1,0:T(8,128)}) custom-call(bf16[256,768]{1,0:T(8,128)(2,1)} %bitcast.3, bf16[128,768]{1,0:T(8,128)(2,1)} %bitcast.4, f32[768]{0:T(1024)} %gain_hbm.1, bf16[768,512]{1,0:T(8,128)(2,1)} %wq_hbm.1, bf16[768,512]{1,0:T(8,128)(2,1)} %wk_hbm.1, bf16[768,512]{1,0:T(8,128)(2,1)} %wv_hbm.1, ...), custom_call_target="tpu_custom_call" | custom-call | tf_op jit(solution)/shard_map/pallas_call | solution.py:544
  88.7 1.8 %shard_map.96 = (bf16[1,128,768]{2,1,0:T(8,128)(2,1)}, f32[3,24,768]{2,1,0:T(8,128)}) custom-call(bf16[128,768]{1,0:T(8,128)(2,1)} %get-tuple-element.4.fg_in, f32[3,24,768]{2,1,0:T(8,128)} %get-tuple-element.5.cg_in), custom_call_target="tpu_custom_call" | custom-call | tf_op jit(solution)/shard_map/pallas_call | solution.py:617

commit v5 on v4

--- a/solution.py
+++ b/solution.py
@@ -17,14 +17,14 @@
 TOK, CH, HEADS, HS = 128, 768, 4, 128
 QROWS = 512
 SPAN = CH // (NX * NY)
-PAD = 80
 HALF = CH // 2
 QUARTER = CH // NX
 TILES = (
-    ((False, 0), (False, 1), (True, 0), (True, 3), (True, 6)),
-    ((False, 2), (False, 3), (False, 4), (True, 1), (True, 4)),
-    ((False, 5), (False, 6), (False, 7), (True, 2), (True, 5)),
+    ((False, 0), (False, 1), (False, 2), (True, 3)),
+    ((False, 3), (False, 4), (True, 0), (True, 2), (True, 5)),
+    ((False, 5), (False, 6), (True, 1), (True, 4), (True, 6)),
 )
+N_TILES = 7
 
 
 def unit_rows(raw):
@@ -38,7 +38,7 @@
 
 def kernel(
     rows_hbm, feat_hbm, gain_hbm, wq_hbm, wk_hbm, wv_hbm, temper_hbm, hg_hbm,
-    fg_out, cg_out,
+    fg_out, own_out, twin_out,
     rows_ref, feat_ref, gain_ref, wq_ref, wk_ref, wv_ref, temper_ref, hg_ref, prev, outgoing, keys, vals, qg, raw, wt, wbuf, e_buf, gp_buf, dv, dk, sib_v, sib_k, st_v, st_k, in_v, in_k,
     total, back, dall, fgs, fgb, tiles_y, tiles_z, yb1, zb1, s1, s2, zb2, yb2, fin, fin_sib,
     prev_sem, a_send, a_recv, k_send, k_recv, w_send, w_recv, sv_send, sv_recv, sk_send, sk_recv,
@@ -223,9 +223,9 @@
     sends += start_heads(1, qg.at[0, slot_rows])
     ring_own(0, 2)
     ring_own(0, 3)
+    sends += start_heads(3, qg.at[1, slot_rows])
     ring_own(1, 0)
     ring_own(1, 1)
-    sends += start_heads(3, qg.at[1, slot_rows])
     ring_own(1, 2)
     ring_own(1, 3)
     ring_on(0)
@@ -239,6 +239,11 @@
         expo = jnp.exp2(scores * (factor * math.log2(math.e)))
         e_buf[block] = expo
         return exp_sum + jnp.sum(expo, axis=0, keepdims=True)
+
+    def prob_grad(block, dot_sum):
+        grad_prob = lax.dot_general(vals[block], qg[1], LAST_BOTH, preferred_element_type=F32)
+        gp_buf[block] = grad_prob
+        return dot_sum + jnp.sum(e_buf[block] * grad_prob, axis=0, keepdims=True)
 
     exp_sum = score_pass(me, jnp.zeros((1, QROWS), F32))
     got_twin(0)
@@ -252,30 +257,27 @@
     got_from_twin(0, 1)
     exp_sum = score_pass(twin_right, exp_sum)
     exp_sum = score_pass(from_far, exp_sum)
+    for j in range(4):
+        arrived(qg.at[1, pl.ds(j * TOK, TOK)], a_recv.at[3, j])
+    dot_sum = prob_grad(me, jnp.zeros((1, QROWS), F32))
+    got_twin(1)
+    dot_sum = prob_grad(twin_me, dot_sum)
     got_from_twin(0, 2)
     exp_sum = score_pass(twin_far, exp_sum)
     inv_sum = 1.0 / exp_sum
 
-    for j in range(4):
-        arrived(qg.at[1, pl.ds(j * TOK, TOK)], a_recv.at[3, j])
     order = (xo, xr, xl, x)
     to = (far, right, left)
 
     def value_grad(block):
         prob = (e_buf[block] * inv_sum).astype(BF16)
         dv[block] = jnp.dot(prob, qg[1], preferred_element_type=F32).astype(BF16)
-
-    def prob_grad(block, dot_sum):
-        grad_prob = lax.dot_general(vals[block], qg[1], LAST_BOTH, preferred_element_type=F32)
-        gp_buf[block] = grad_prob
-        return dot_sum + jnp.sum(e_buf[block] * grad_prob, axis=0, keepdims=True)
 
     def pass_values(i):
         arrived(sib_v.at[i], sv_recv.at[i])
         st_v[i] = (dv[2 * order[i] + core].astype(F32) + sib_v[i].astype(F32)).astype(BF16)
         send(st_v.at[i], in_v.at[i], mv_send.at[i], mv_recv.at[i], to[i])
 
-    dot_sum = jnp.zeros((1, QROWS), F32)
     for i in range(NX):
         block = 2 * order[i] + 1 - core
         value_grad(block)
@@ -283,11 +285,8 @@
         value_grad(2 * order[i] + core)
         if i > 1:
             pass_values(i - 2)
-    dot_sum = prob_grad(me, dot_sum)
+    dot_sum = prob_grad(from_left, dot_sum)
     pass_values(2)
-    got_twin(1)
-    dot_sum = prob_grad(twin_me, dot_sum)
-    dot_sum = prob_grad(from_left, dot_sum)
     dot_sum = prob_grad(from_right, dot_sum)
     ring_far(1)
     for k, other in enumerate((twin_left, twin_right)):
@@ -338,22 +337,24 @@
             start_back(2, j)
 
     grad_query = jnp.zeros((HS, QROWS), F32)
-    pending = None
+    pending = []
     for half in range(2):
         for i in range(NX):
             block = 2 * order[i] + 1 - core
             grad_query = key_grad(block, half, grad_query)
             send(half_of(dk, block, half), half_of(sib_k, i, half), sk_send.at[half, i], sk_recv.at[half, i], twin)
             grad_query = key_grad(2 * order[i] + core, half, grad_query)
-            if pending is not None and pending[1] < 3:
-                pass_keys(*pending)
-            pending = (half, i)
-            if pending == (1, 2):
-                finish_values()
+            if i < 3:
+                pending.append((half, i))
+            if len(pending) > 2:
+                pass_keys(*pending.pop(0))
+    for one in pending:
+        pass_keys(*one)
     total[0] = jnp.transpose(grad_query).astype(BF16)
 
     for j in range(4):
         start_back(0, j)
+    finish_values()
     for half in range(2):
         low = half * half_rows
         high = low + half_rows
@@ -418,22 +419,28 @@
         arrived(g_slot(k, xr, 1), g_recv.at[k, 3])
         send(g_slot(k, xr, 1), g_slot(k, xr, 1), g_send.at[k, 6], g_recv.at[k, 5], left)
 
-    def sum_chunk(k):
+    def sum_chunk(k, before):
         arrived(g_slot(k, xl, 1), g_recv.at[k, 1])
         arrived(g_slot(k, xr, 0), g_recv.at[k, 2])
         arrived(g_slot(k, x, 1 - core), g_recv.at[k, 6])
         arrived(g_slot(k, xo, 0), g_recv.at[k, 4])
         arrived(g_slot(k, xo, 1), g_recv.at[k, 5])
         terms = jnp.dot(wbuf[...].reshape(3 * QUARTER, 8 * TOK), fgb[k], preferred_element_type=F32) * (1.0 / (2 * NZ))
+        after = []
         for b in range(NY):
             taps = [terms[i * QUARTER + b * SPAN : i * QUARTER + (b + 1) * SPAN] for i in range(3)]
-            rows = jnp.concatenate(taps + [jnp.zeros((PAD - 3 * SPAN, 128), F32)], axis=0).astype(BF16)
-            for i, (by_z, at_tile) in enumerate(TILES[k]):
-                tile = rows[16 * i : 16 * (i + 1)]
+            rows = jnp.concatenate(taps, axis=0)
+            tiles = [rows[16 * i : 16 * (i + 1)] for i in range(4)]
+            after.append(rows[64:72])
+            if k == 1:
+                tiles.append(jnp.concatenate([before[b], rows[64:72]], axis=0))
+            elif k == 2:
+                tiles.append(jnp.concatenate([rows[64:72], jnp.zeros((8, 128), F32)], axis=0))
+            for tile, (by_z, at_tile) in zip(tiles, TILES[k]):
                 if by_z:
-                    tiles_z[at_tile, b] = tile
+                    tiles_z[at_tile, b] = tile.astype(BF16)
                 else:
-                    tiles_y[b, at_tile] = tile
+                    tiles_y[b, at_tile] = tile.astype(BF16)
         of_y = [at_tile for by_z, at_tile in TILES[k] if not by_z]
         some = pl.ds(of_y[0], len(of_y))
         for i in range(1, NY):
@@ -451,6 +458,8 @@
                 def _():
                     zb1[z] = tiles_z[at_tile]
 
+        return after
+
     def to_owner(at_tile):
         return copy(tiles_z.at[at_tile], zb1.at[z], tz_send.at[at_tile], tz_recv.at[z], (seq, 2 * at_tile + core))
 
@@ -468,17 +477,18 @@
     gather_on(1)
     got_windows(0, 1, 2)
     got_windows(1, 0, 1)
-    sum_chunk(0)
+    halves = sum_chunk(0, None)
     arrived(g_slot(2, xl, 0), g_recv.at[2, 0])
     arrived(g_slot(2, xr, 1), g_recv.at[2, 3])
-    sum_chunk(1)
-    sum_chunk(2)
+    sum_chunk(1, halves)
+    sum_chunk(2, None)
     for i in range(1, NY):
         from_y = lax.rem(y + i, NY)
         for k in range(3):
             of_y = [at_tile for by_z, at_tile in TILES[k] if not by_z]
             arrived(yb1.at[from_y, pl.ds(of_y[0], len(of_y))], t_recv.at[k, from_y])
-    s1[...] = added(yb1).astype(BF16)
+    s1[0:N_TILES] = added(yb1).astype(BF16)
+    s1[N_TILES] = jnp.zeros((16, 128), BF16)
     for i in range(1, 8):
         to_z = lax.rem(z + i, NZ)
         send(s1.at[to_z], zb2.at[z], u_send.at[0, i], u_recv.at[0, z], on_z[i - 1])
@@ -510,15 +520,8 @@
         arrived(fin.at[from_z], f_recv.at[from_z])
     send(fin, fin_sib, c_sem.at[0], c_sem.at[1], twin)
     arrived(fin_sib, c_sem.at[1])
-    for half in range(2):
-        mine = jnp.where(core == half, fin[...].astype(F32), fin_sib[...].astype(F32))
-        wide = []
-        for i in range(PAD // 16):
-            row = [TILES[k][i] for k in range(3)]
-            wide.append(jnp.concatenate([mine[at_tile, int(by_z)] for by_z, at_tile in row], axis=1))
-        wide = jnp.concatenate(wide, axis=0)
-        for k in range(3):
-            cg_out[k, :, half * HALF : (half + 1) * HALF] = wide[k * SPAN : (k + 1) * SPAN]
+    own_out[...] = fin[...]
+    twin_out[...] = fin_sib[...]
 
     for one in sends:
         one.wait_send()
@@ -529,9 +532,17 @@
             to_owner(at_tile).wait_send()
 
 
-def publish(fg_in, cg_in, fg_out, cg_out):
+def publish(fg_in, own, twin, fg_out, cg_out):
     fg_out[0] = fg_in[...]
-    cg_out[...] = cg_in[...]
+    core = lax.rem(lax.axis_index("dp"), 2)
+    for half in range(2):
+        mine = jnp.where(core == half, own[...].astype(F32), twin[...].astype(F32))
+        tiles = [[mine[at_tile, int(by_z)] for by_z, at_tile in row] for row in TILES]
+        last = (tiles[1][4][0:8], tiles[1][4][8:16], tiles[2][4][0:8])
+        wide = [jnp.concatenate([tiles[k][i] for k in range(3)], axis=1) for i in range(4)]
+        wide = jnp.concatenate(wide + [jnp.concatenate(last, axis=1)], axis=0)
+        for k in range(3):
+            cg_out[k, :, half * HALF : (half + 1) * HALF] = wide[k * SPAN : (k + 1) * SPAN]
 
 
 def on_device(input_rows, features, norm_gain, w_query, w_key, w_value, temper, head_grads):
@@ -541,14 +552,15 @@
     def scratch(*shape, dtype=BF16):
         return pltpu.VMEM(shape, dtype)
 
-    fg, cg = pl.pallas_call(
+    results = pl.pallas_call(
         kernel,
         out_shape=(
             jax.ShapeDtypeStruct((TOK, CH), BF16),
-            jax.ShapeDtypeStruct((3, SPAN, CH), F32),
+            jax.ShapeDtypeStruct((NZ, 2, 16, 128), BF16),
+            jax.ShapeDtypeStruct((NZ, 2, 16, 128), BF16),
         ),
         in_specs=[hbm] * 8,
-        out_specs=(vmem, vmem),
+        out_specs=(vmem, vmem, vmem),
         scratch_shapes=[
             scratch(2 * TOK, CH),
             scratch(TOK, CH),
@@ -581,9 +593,9 @@
             scratch(3, TOK, HEADS * HS),
             scratch(2, 3, TOK, 128),
             scratch(3, 8 * TOK, 128),
-            scratch(NY, 8, 16, 128),
-            scratch(NZ, NY, 16, 128),
-            scratch(NY, 8, 16, 128),
+            scratch(NY, N_TILES, 16, 128),
+            scratch(N_TILES, NY, 16, 128),
+            scratch(NY, N_TILES, 16, 128),
             scratch(NZ, 8, 16, 128),
             scratch(8, 16, 128),
             scratch(8, 16, 128),
@@ -620,9 +632,9 @@
             jax.ShapeDtypeStruct((1, TOK, CH), BF16),
             jax.ShapeDtypeStruct((3, SPAN, CH), F32),
         ),
-        in_specs=[vmem, vmem],
+        in_specs=[vmem, vmem, vmem],
         out_specs=(vmem, vmem),
-    )(fg, cg)
+    )(*results)
 
 
 def solution(mesh):

time: 90.7 us -> 89.9 us (level)
  no operation moved by 1% of the time
where the time goes in v5:
time: 89.9 us; the launch traced here: 89.7 us
  Pallas kernels  89.1 us (99%)
    pallas_call x1, Pallas kernels, on_device(): pl.pallas_call(kernel, out_shape=(jax.ShapeDtypeStruct((TOK, CH), BF16),...  87.3 us

profile of v5, /device:TPU:1, one launch (start us, length us, event | category | flops | bytes accessed | tf_op | source)
XLA Modules:
  0.0 89.7 jit_solution(11442193568744645729)
XLA Ops:
  0.6 87.3 %shard_map.95 = (bf16[128,768]{1,0:T(8,128)(2,1)}, bf16[8,2,16,128]{3,2,1,0:T(8,128)(2,1)}, bf16[8,2,16,128]{3,2,1,0:T(8,128)(2,1)}) custom-call(bf16[256,768]{1,0:T(8,128)(2,1)} %bitcast.3, bf16[128,768]{1,0:T(8,128)(2,1)} %bitcast.4, f32[768]{0:T(1024)} %gain_hbm.1, bf16[768,512]{1,0:T(8,128)(2,1)} %wq_hbm.1, bf16[768,512]{1,0:T(8,128)(2,1)} %wk_hbm.1, ...), custom_call_target="tpu_custom_call" | custom-call | tf_op jit(solution)/shard_map/pallas_call | solution.py:555
  88.0 1.7 %shard_map.96 = (bf16[1,128,768]{2,1,0:T(8,128)(2,1)}, f32[3,24,768]{2,1,0:T(8,128)}) custom-call(bf16[128,768]{1,0:T(8,128)(2,1)} %get-tuple-element.5.fg_in, bf16[8,2,16,128]{3,2,1,0:T(8,128)(2,1)} %get-tuple-element.6.own, bf16[8,2,16,128]{3,2,1,0:T(8,128)(2,1)} %get-tuple-element.7.twin), custom_call_target="tpu_custom_call" | custom-call | tf_op jit(solution)/shard_map/pallas_call | solution.py:629
